TPU v7x, 256 devices: a whole 4x4x8 slice. The times are simulated.
256 devices in a mesh: lat: 8 (over y, core), wave: 16 (over x_lo, z), lev: 2 (over x_hi).
Axes of the slice: x: 4 (x_hi: 2, x_lo: 2; x = x_hi * 2 + x_lo), y: 4, z: 8, core: 2. Of those that a mesh axis runs over, the one named last changes fastest.
Arguments:
- fourier: bfloat16 [512, 2048, 256], P('wave', 'lat', 'lev'), may hold values from -6 to 6
- legendre: bfloat16 [512, 1024, 2, 1024], P('wave', 'lat', None, 'lev'), may hold values from -0.1875 to 0.1875
- wave_list: int32 [512], P('wave'), may hold values from 0 to 511, as said below
Outputs:
- spectra: bfloat16 [2, 512, 2, 512, 256], P(None, 'lat', None, 'wave', 'lev')
Inputs may be any that keep to these rules, and one draw needn't show every extreme that they name: `wave_list`: A permutation of the slots; read in blocks of 32 entries, the entries k * 2 to (k + 1) * 2 - 1 of every block lie in k * 32 to (k + 1) * 32 - 1.
All inputs are finite; a program needn't handle non-finite values.
Results may differ from a plain program's by a relative error of at most 0.017.
Values may be sent and summed in bfloat16 or wider, within the bound.
No kernel may reach another device: no remote copies, remote signals or barrier semaphores. Data moves between devices by JAX's collectives and lax.ppermute only.
A program may use at most 128 MiB of HBM per device.

v0:
```python
import jax
import jax.numpy as jnp
from jax import lax
from jax.sharding import PartitionSpec as P

NN = 2048


def swapped(array, axis, stride):
    return lax.ppermute(array, axis, [(i, i ^ 1 << stride) for i in range(lax.axis_size(axis))])


def degree_terms(folded_sum, folded_diff, parity, table_part):
    results = []
    for degree_parity in range(2):
        pick = ((parity + degree_parity) % 2 == 0)[:, None, None]
        source = jnp.where(pick, folded_sum, folded_diff)
        results.append(
            jnp.einsum(
                "slq,slc->qsc",
                table_part[:, :, degree_parity, :],
                source,
                preferred_element_type=jnp.float32,
            )
        )
    return jnp.stack(results, axis=1)


def degree_mask(slot_ids, first_q, q_count, stride):
    q_index = first_q + jnp.arange(q_count, dtype=jnp.int32)
    degrees = 2 * q_index[:, None] + jnp.arange(2, dtype=jnp.int32)[None, :]
    lowest = slot_ids * stride + slot_ids % 2 * (stride - 1)
    return degrees[:, :, None] >= lowest[None, None, :]


def shards(fourier, legendre, wave_list):
    block_count = lax.axis_size("wave")
    block_id = lax.axis_index("wave")
    slot_count = fourier.shape[0]
    per_block = slot_count // block_count
    stride = NN // (slot_count * block_count)
    listing = lax.all_gather(wave_list, "wave", axis=0, tiled=True)
    listing_grid = listing.reshape(block_count, block_count, per_block)
    column = lax.dynamic_index_in_dim(listing_grid, block_id, axis=1, keepdims=False)
    local_rows = (column - block_id * slot_count).reshape(-1)
    outgoing = jnp.take(fourier, local_rows, axis=0)
    arrived = lax.all_to_all(outgoing, "wave", split_axis=0, concat_axis=0, tiled=True)
    half_rows = arrived.shape[1] // 2
    own_rows = arrived[:, :half_rows]
    remote_rows = arrived[:, half_rows:][:, ::-1]
    bit_count = lax.axis_size("lat").bit_length() - 1
    bit_order = list(range(bit_count))
    for bit_index in bit_order:
        remote_rows = swapped(remote_rows, "lat", bit_index)
    near_rows = own_rows.astype(jnp.float32)
    mirrored = remote_rows.astype(jnp.float32)
    folded_sum = (near_rows + mirrored).astype(jnp.bfloat16)
    folded_diff = (near_rows - mirrored).astype(jnp.bfloat16)
    parity = wave_list % 2
    whole_table = lax.all_gather(legendre, "lev", axis=3, tiled=True)
    partials = degree_terms(folded_sum, folded_diff, parity, whole_table)
    q_total = partials.shape[0]
    shaped = partials.reshape(2, q_total // 2, 2, slot_count, partials.shape[3])
    summed = lax.psum_scatter(
        shaped.astype(jnp.bfloat16), "lat", scatter_dimension=1, tiled=True
    ).astype(jnp.float32)
    piece_rows = summed.shape[1]
    first_q = lax.axis_index("lat") * piece_rows
    keep_masks = jnp.stack(
        [
            degree_mask(wave_list, half_index * (q_total // 2) + first_q, piece_rows, stride)
            for half_index in range(2)
        ]
    )
    return jnp.where(keep_masks[..., None], summed, 0.0).astype(jnp.bfloat16)


def solution(mesh):
    placed = (P("wave", "lat", "lev"), P("wave", "lat", None, "lev"), P("wave"))
    return jax.shard_map(
        shards,
        mesh=mesh,
        in_specs=placed,
        out_specs=P(None, "lat", None, "wave", "lev"),
        check_vma=False,
    )
```

profile of v0, /device:TPU:1, one launch (start us, length us, event | category | flops | bytes accessed | tf_op | source)
XLA Modules:
  0.0 420.7 jit_solution(13651533313590179761)
XLA Ops:
  6.5 0.0 copy-start
  6.5 0.0 all-gather.2.cloned.1.call-start
  6.5 8.7 %copy.15 = bf16[32,128,2,512]{3,1,0,2:T(8,128)(2,1)} copy(bf16[32,128,2,512]{3,2,1,0:T(2,128)(2,1)} %param.4) | data formatting | bytes 16777216 | tf_op args[1]
  15.2 0.0 copy-start.3
  15.2 0.0 copy-start.2
  15.2 0.0 all-gather.2.cloned.1.call-update
  15.3 0.0 reduce-scatter.5.cloned.1.call-start
  15.3 0.6 copy-done.3
  15.9 0.6 dynamic-slice
  17.2 0.0 copy-done.2
  17.2 0.2 dynamic-update-slice
  17.4 0.1 reshape.103
  17.6 56.7 %all-reduce.1 = s32[16,16,2]{2,1,0:T(8,128)S(1)} all-reduce(s32[16,16,2]{2,1,0:T(8,128)S(1)} %reshape.103), channel_id=1, replica_groups=mesh['lat'=8,'wave'=16,'lev'=2] {'wave'}, use_global_device_ids=true, to_apply=%add | all-reduce | flops 512 | bytes 4096
  74.3 0.5 broadcast.160
  74.8 0.7 fusion.18
  75.5 0.1 sub.28
  75.6 0.1 sub.27
  75.7 0.0 copy-done
  75.7 2.1 gather_fusion
  77.9 1.8 broadcast_select_fusion
  79.7 37.7 %all_to_all.5 = bf16[32,256,128]{2,1,0:T(8,128)(2,1)S(1)} all-to-all(bf16[32,256,128]{2,1,0:T(8,128)(2,1)S(1)} %broadcast_select_fusion), channel_id=1, replica_groups=mesh['lat'=8,'wave'=16,'lev'=2] {'wave'}, dimensions={0} | all-to-all | bytes 4194304 | tf_op jit(solution)/shard_map/all_to_all | solution.py:47
  117.4 0.1 slice.19
  117.5 10.1 %rev.3 = bf16[32,128,128]{2,1,0:T(8,128)(2,1)} reverse(bf16[32,128,128]{2,1,0:T(8,128)(2,1)S(1)} %slice.19), dimensions={1} | reverse | bytes 2097152 | tf_op jit(solution)/shard_map/rev | solution.py:50
  127.6 15.2 %collective-permute-start = (bf16[32,128,128]{2,1,0:T(8,128)(2,1)}, bf16[32,128,128]{2,1,0:T(8,128)(2,1)S(1)}, u32[]{:S(2)}, u32[]{:S(2)}) collective-permute-start(bf16[32,128,128]{2,1,0:T(8,128)(2,1)} %rev.3), channel_id=1, source_target_pairs={{0,32},{32,0},{64,96},{96,64},{128,160},{160,128},{192,224},{224,1... | collective-permute-start | bytes 3145736 | tf_op jit(solution)/shard_map/ppermute | solution.py:10
  142.8 2.5 collective-permute-done
  145.3 1.3 collective-permute-start.1
  146.6 23.2 %collective-permute-done.1 = bf16[32,128,128]{2,1,0:T(8,128)(2,1)S(1)} collective-permute-done((bf16[32,128,128]{2,1,0:T(8,128)(2,1)S(1)}, bf16[32,128,128]{2,1,0:T(8,128)(2,1)S(1)}, u32[]{:S(2)}, u32[]{:S(2)}) %collective-permute-start.1) | collective-permute-done | bytes 1048608 | tf_op jit(solution)/shard_map/ppermute | solution.py:10
  169.7 2.9 collective-permute-start.2
  172.7 22.2 %collective-permute-done.2 = bf16[32,128,128]{2,1,0:T(8,128)(2,1)S(1)} collective-permute-done((bf16[32,128,128]{2,1,0:T(8,128)(2,1)S(1)}, bf16[32,128,128]{2,1,0:T(8,128)(2,1)S(1)}, u32[]{:S(2)}, u32[]{:S(2)}) %collective-permute-start.2) | collective-permute-done | bytes 1048608 | tf_op jit(solution)/shard_map/ppermute | solution.py:10
  194.9 54.2 %all-gather.2.cloned.1.call-done = bf16[32,128,2,1024]{3,1,0,2:T(8,128)(2,1)} async-done(((bf16[32,128,2,512]{3,1,0,2:T(8,128)(2,1)}), bf16[32,128,2,1024]{3,1,0,2:T(8,128)(2,1)}) %all-gather.2.cloned.1.call-update) | async-done | bytes 16777232 | tf_op jit(solution)/shard_map/all_gather | solution.py:60
  249.1 9.1 %convert_bitcast_fusion.1 = bf16[1024,32,128]{0,2,1:T(8,128)(2,1)} fusion(bf16[32,128,2,1024]{3,1,0,2:T(8,128)(2,1)} %all-gather.2.cloned.1.call-done, pred[32]{0:T(512)(128)(4,1)S(1)} %get-tuple-element.11, bf16[32,128,128]{2,1,0:T(8,128)(2,1)S(1)} %collective-permute-done.2, bf16[32,256,128]{2,1,0:T(8,128)(2,1)S(1)} %all_to_all.5), kind=kOutput, calls=%fused_computation.8 | convolution fusion | flops 1081606144 | bytes 18874880 | tf_op jit(solution)/shard_map/slq,slc->qsc/dot_general | solution.py:19
  258.2 12.5 %copy.22 = bf16[1024,32,128]{2,1,0:T(8,128)(2,1)} copy(bf16[1024,32,128]{0,2,1:T(8,128)(2,1)} %convert_bitcast_fusion.1) | data formatting | bytes 16777216 | tf_op jit(solution)/shard_map/stack | solution.py:26
  270.6 9.1 %convert_bitcast_fusion = bf16[1024,32,128]{0,2,1:T(8,128)(2,1)} fusion(bf16[32,128,2,1024]{3,1,0,2:T(8,128)(2,1)} %all-gather.2.cloned.1.call-done, pred[32]{0:T(512)(128)(4,1)S(1)} %get-tuple-element.12, bf16[32,128,128]{2,1,0:T(8,128)(2,1)S(1)} %collective-permute-done.2, bf16[32,256,128]{2,1,0:T(8,128)(2,1)S(1)} %all_to_all.5), kind=kOutput, calls=%fused_computation.7 | convolution fusion | flops 1081606144 | bytes 18874880 | tf_op jit(solution)/shard_map/slq,slc->qsc/dot_general | solution.py:19
  279.7 12.5 %copy.23 = bf16[1024,32,128]{2,1,0:T(8,128)(2,1)} copy(bf16[1024,32,128]{0,2,1:T(8,128)(2,1)} %convert_bitcast_fusion) | data formatting | bytes 16777216 | tf_op jit(solution)/shard_map/stack | solution.py:26
  292.2 8.0 %pad_maximum_fusion = bf16[2,512,2,32,128]{4,3,2,1,0:T(8,128)(2,1)S(1)} fusion(bf16[2,512,1,32,128]{4,3,2,1,0:T(8,128)(2,1)} %bitcast.36, bf16[2,512,1,32,128]{4,3,2,1,0:T(8,128)(2,1)} %bitcast.35), kind=kLoop, calls=%fused_computation.2 | loop fusion | flops 8388608 | bytes 33554432 | tf_op jit(solution)/shard_map/stack | solution.py:26
  300.2 2.0 copy.24
  302.2 15.3 %copy.30 = bf16[64,8,128,128]{3,1,2,0:T(8,128)(2,1)} copy(bf16[64,8,128,128]{3,2,1,0:T(8,128)(2,1)S(1)} %bitcast.34) | data formatting | bytes 33554432
  317.4 0.0 reduce-scatter.5.cloned.1.call-update
  317.5 0.1 broadcast_compare_fusion.1
  317.6 0.2 copy.14
  317.8 91.1 %reduce-scatter.5.cloned.1.call-done = bf16[64,16384]{1,0:T(8,128)(2,1)} async-done(((bf16[512,16384]{1,0:T(8,128)(2,1)}), bf16[64,16384]{1,0:T(8,128)(2,1)}) %reduce-scatter.5.cloned.1.call-update) | async-done | bytes 2097168
  408.9 0.0 copy-start.1
  408.9 2.3 copy.27
  411.2 2.6 select_convert_fusion
  413.8 0.0 copy-done.1
  (10 shorter events, 0.1 us)
Async XLA Ops:
  6.5 69.2 %copy-start = (bf16[32,256,128]{2,1,0:T(8,128)(2,1)S(1)}, bf16[32,256,128]{2,1,0:T(8,128)(2,1)}, u32[]{:S(2)}) copy-start(bf16[32,256,128]{2,1,0:T(8,128)(2,1)} %param.3) | copy-start | bytes 6291460
  6.5 242.6 %all-gather.2.cloned.1.call-start = ((), (), s32[]{:S(2)}) async-start(), calls=%async_computation.2 | async-start | bytes 25165824 | tf_op jit(solution)/shard_map/all_gather | solution.py:60
  15.2 0.7 copy-start.3
  15.2 1.9 copy-start.2
  15.3 393.6 %reduce-scatter.5.cloned.1.call-start = ((), (), s32[]{:S(2)}) async-start(), calls=%async_computation.3 | async-start | bytes 18874368
  127.6 17.7 %collective-permute-start = (bf16[32,128,128]{2,1,0:T(8,128)(2,1)}, bf16[32,128,128]{2,1,0:T(8,128)(2,1)S(1)}, u32[]{:S(2)}, u32[]{:S(2)}) collective-permute-start(bf16[32,128,128]{2,1,0:T(8,128)(2,1)} %rev.3), channel_id=1, source_target_pairs={{0,32},{32,0},{64,96},{96,64},{128,160},{160,128},{192,224},{224,1... | collective-permute-start | bytes 3145736 | tf_op jit(solution)/shard_map/ppermute | solution.py:10
  145.3 24.5 %collective-permute-start.1 = (bf16[32,128,128]{2,1,0:T(8,128)(2,1)S(1)}, bf16[32,128,128]{2,1,0:T(8,128)(2,1)S(1)}, u32[]{:S(2)}, u32[]{:S(2)}) collective-permute-start(bf16[32,128,128]{2,1,0:T(8,128)(2,1)S(1)} %collective-permute-done), channel_id=1, source_target_pairs={{0,64},{32,96},{64,0},{96,32},{128,192},{160,224},{192,128},{224,1... | collective-permute-start | bytes 3145736 | tf_op jit(solution)/shard_map/ppermute | solution.py:10
  169.7 25.2 %collective-permute-start.2 = (bf16[32,128,128]{2,1,0:T(8,128)(2,1)S(1)}, bf16[32,128,128]{2,1,0:T(8,128)(2,1)S(1)}, u32[]{:S(2)}, u32[]{:S(2)}) collective-permute-start(bf16[32,128,128]{2,1,0:T(8,128)(2,1)S(1)} %collective-permute-done.1), channel_id=1, source_target_pairs={{0,128},{32,160},{64,192},{96,224},{128,0},{160,32},{192,64},{224,... | collective-permute-start | bytes 3145736 | tf_op jit(solution)/shard_map/ppermute | solution.py:10
  408.9 5.0 %copy-start.1 = (bf16[32,256,128]{2,1,0:T(8,128)(2,1)S(1)}, bf16[32,256,128]{2,1,0:T(8,128)(2,1)}, u32[]{:S(2)}) copy-start(bf16[32,256,128]{2,1,0:T(8,128)(2,1)} %param.3) | copy-start | bytes 6291460
Sparse Core Ops, SparseCore 0:
  15.4 233.6 all-gather.1
  317.6 91.2 reduce-scatter.4
where the time goes:
time: 422 us; the launch traced here: 421 us
  waiting for transfers between devices  193 us (46%)
  blocking collectives  94.4 us (22%)
  local copies, waits for them, and re-layouts  68 us (16%)
  starting transfers between devices  19.4 us (5%)
  matrix products  18.1 us (4%)
  between operations  14.2 us (3%)
  other arithmetic  13.3 us (3%)
    unnamed x3, waiting for transfers between devices  91.1 us
    unnamed x1, blocking collectives  56.7 us
    all_gather x1, waiting for transfers between devices, shards(): whole_table = lax.all_gather(legendre, 'lev', axis=3, tiled=True)  54.2 us
    ppermute x3, waiting for transfers between devices, swapped(): lax.ppermute(array, axis, [(i, i ^ 1 << stride) for i in range(lax.axis_s...  47.9 us
    all_to_all x1, blocking collectives, shards(): lax.all_to_all(outgoing, 'wave', split_axis=0, concat_axis=0, tiled=True)  37.7 us
    unnamed x15, local copies, waits for them, and re-layouts  29.7 us
    another operation x2, local copies, waits for them, and re-layouts, degree_terms(): return jnp.stack(results, axis=1)  25 us
    ppermute x3, starting transfers between devices, swapped(): lax.ppermute(array, axis, [(i, i ^ 1 << stride) for i in range(lax.axis_s...  19.4 us
  transfers between devices with their start and end apart: 5, of which 5 were waited for; matrix products, arithmetic and copies ran while one was open for 4% of the time, Pallas kernels for 0%

commit v1 on v0

v1 whole, which is shorter than its diff:
```python
import functools

import jax
import jax.numpy as jnp
from jax import lax
from jax.experimental import pallas as pl
from jax.experimental.pallas import tpu as pltpu
from jax.sharding import PartitionSpec as P

NN = 2048
FIRST = (2, 6, 4)
LAST = (3, 7, 5, 1)


def after(first, *arrays):
    return lax.optimization_barrier((first, *arrays))[1:]


def first_kernel(place, table, *outs):
    for out, hop in zip(outs, FIRST):
        band = place[0] ^ hop
        out[0] = table[band]
        out[1] = table[15 - band]


def rest_kernel(place, table, wide, slim, *outs):
    lat, lev = place[0], place[1]
    reach, cut, end = table.shape[3], wide.shape[3], slim.shape[3]

    def lone(out, band):
        @pl.when(lev == 0)
        def _():
            out[:, :, 0 : reach - cut] = jnp.zeros_like(out[:, :, 0 : reach - cut])

            @pl.when(band < 4)
            def _():
                out[:, :, reach - cut :] = wide[band]

            @pl.when(band >= 4)
            def _():
                out[:, :, reach - cut : reach - end] = jnp.zeros_like(slim[0])
                out[:, :, reach - end :] = slim[band - 4]

        @pl.when(lev != 0)
        def _():
            out[...] = table[16 + band]

    for out, hop in zip(outs[:3], FIRST):
        lone(out, lat ^ hop)
    for out, hop in zip(outs[3:], (0, *LAST)):
        band = lat ^ hop
        out[0] = table[band]
        out[1] = table[15 - band]
        lone(out.at[2], band)


def transform_kernel(place, *refs):
    first, lone, whole, arrived, out, source, table, fields, sems = refs[:3], refs[3:6], refs[6:11], *refs[11:]
    lat = place[0]
    rows, reach = table.shape[2] // 8, table.shape[3]
    width = reach // 4
    half = width // 2
    cols = fields.shape[3]
    fetch = [pltpu.make_async_copy(arrived, fields, sems.at[11])]
    spans = {hop: pl.ds(hop * rows, rows) for hop in range(8)}
    for n, hop in enumerate(FIRST):
        fetch.append(pltpu.make_async_copy(first[n], table.at[0:2, :, spans[hop]], sems.at[n]))
        fetch.append(pltpu.make_async_copy(lone[n], table.at[2, :, spans[hop]], sems.at[3 + n]))
    for n, hop in enumerate((0, *LAST)):
        fetch.append(pltpu.make_async_copy(whole[n], table.at[:, :, spans[hop]], sems.at[6 + n]))
    for copy in fetch:
        copy.start()
    at_row = lax.broadcasted_iota(jnp.int32, (rows, rows), 0)
    at_col = lax.broadcasted_iota(jnp.int32, (rows, rows), 1)
    flip = (at_row + at_col == rows - 1).astype(jnp.bfloat16)
    fetch[0].wait()
    pairs = [(f, v) for f in range(3) for v in range(2)]
    for hop in range(8):
        band = lat ^ hop
        near = [fields[2 * band + v, f, 0:rows, :] for f, v in pairs]
        far = [fields[2 * (7 - band) + v, f, rows : 2 * rows, :] for f, v in pairs]
        mirrored = jnp.dot(flip, jnp.concatenate(far, 1), preferred_element_type=jnp.float32)
        for n, (f, v) in enumerate(pairs):
            one = near[n].astype(jnp.float32)
            other = mirrored[:, n * cols : (n + 1) * cols]
            odd = place[2 + f] == 1
            other = jnp.where(odd, -other, other)
            here = (slice(hop * rows, (hop + 1) * rows), slice(v * cols, (v + 1) * cols))
            source[f, 0, *here] = (one + other).astype(jnp.bfloat16)
            source[f, 1, *here] = (one - other).astype(jnp.bfloat16)
    for copy in fetch[1:]:
        copy.wait()
    for f in range(3):
        for p in range(2):
            for n in range(4):
                values = lax.dot_general(
                    table[f, p, :, n * width : (n + 1) * width],
                    source[f, p],
                    (((0,), (0,)), ((), ())),
                    preferred_element_type=jnp.float32,
                ).astype(jnp.bfloat16)
                for h in range(2):
                    for v in range(2):
                        out[2 * (2 * n + h) + v, f, p] = values[
                            h * half : (h + 1) * half, v * cols : (v + 1) * cols
                        ]


def pick_kernel(order, arrived, out):
    for n, slot in enumerate(order):
        out[n // 3, n % 3] = arrived[slot]


def spread_kernel(place, lowest, owned, out):
    piece, slots, cols = out.shape[1], out.shape[3], out.shape[4]
    bands = slots // 4
    up = range(bands)
    down = range(bands - 1, -1, -1)
    whole = [
        [(2 * m, 0) for m in up] + [(2 * m, 1) for m in down],
        [(2 * m + 1, 0) for m in up]
        + [(2 * m + 1, 1) for m in down]
        + [(2 * m + 1, 2) for m in up]
        + [(2 * m, 2) for m in up],
    ]
    for k in range(2):
        count = len(whole[k])
        q = lax.broadcasted_iota(jnp.int32, (piece, count, cols), 0) + (8 * k + place[0]) * piece
        for p in range(2):
            held = jnp.stack([owned[n, e, p].astype(jnp.float32) for n, e in whole[k]])
            held = jnp.transpose(held, (1, 0, 2))
            held = jnp.where(2 * q + p >= lowest[0:count][None], held, 0.0)
            out[k, :, p, 0:count] = held.astype(jnp.bfloat16)
            if count < slots:
                out[k, :, p, count:] = jnp.zeros((piece, slots - count, cols), jnp.bfloat16)


def shards(fourier, legendre, wave_list):
    roomy = pltpu.CompilerParams(vmem_limit_bytes=8 * 1024 * 1024)
    any_space = pl.BlockSpec(memory_space=pl.ANY)
    smem = pl.BlockSpec(memory_space=pltpu.SMEM)
    vmem = pl.BlockSpec(memory_space=pltpu.VMEM)
    lat, lev = lax.axis_index("lat"), lax.axis_index("lev")
    block_id = lax.axis_index("wave")
    slot_count, row_count, cols = fourier.shape
    bands, blocks = lax.axis_size("lat"), lax.axis_size("wave")
    rows, reach = legendre.shape[1], legendre.shape[3]
    width = reach // 4
    stride = NN // (slot_count * blocks)

    def hopped(array, hop):
        return lax.ppermute(array, "lat", [(i, i ^ hop) for i in range(bands)])

    def shape_of(*dims):
        return jax.ShapeDtypeStruct(dims, jnp.bfloat16)

    wide = legendre[24:28, :, :, reach // 2 :]
    slim = legendre[28:32, :, :, reach - width :]
    wide, slim, listing, legendre = lax.optimization_barrier((wide, slim, wave_list, legendre))
    wide = lax.ppermute(wide, "lev", [(1, 0)])
    slim = lax.ppermute(slim, "lev", [(1, 0)])

    wanted = lax.all_to_all(listing.reshape(blocks, -1), "wave", 0, 0, tiled=True)
    local = (wanted - block_id * slot_count).reshape(-1)
    outgoing = jnp.take(fourier, local, axis=0, mode="clip")

    place = jnp.stack([lat, lev]).astype(jnp.int32)
    first = pl.pallas_call(
        first_kernel,
        in_specs=[smem, vmem],
        out_specs=[vmem] * 3,
        out_shape=[shape_of(2, rows, 2, reach)] * 3,
        compiler_params=roomy,
    )(place, legendre)
    outgoing, wide, slim, *first = lax.optimization_barrier((outgoing, wide, slim, *first))
    arrived = lax.all_to_all(outgoing, "wave", 0, 0, tiled=True)
    first = [hopped(array, hop) for array, hop in zip(first, FIRST)]
    rest = pl.pallas_call(
        rest_kernel,
        in_specs=[smem] + [vmem] * 3,
        out_specs=[vmem] * 8,
        out_shape=[shape_of(rows, 2, reach)] * 3 + [shape_of(3, rows, 2, reach)] * 5,
        compiler_params=roomy,
    )(place, legendre, wide, slim)
    lone, (mine, *whole) = rest[:3], rest[3:]
    whole = [mine] + [hopped(array, hop) for array, hop in zip(whole, LAST)]
    lone = [hopped(array, hop) for array, hop in zip(lone, FIRST)]
    arrived, first, whole[:3] = lax.optimization_barrier((arrived, first, whole[:3]))

    order = []
    for m in range(bands):
        order += [m, 15 - m, 24 + m, m, 15 - m, 16 + m]
    handled = pl.pallas_call(
        functools.partial(pick_kernel, order),
        in_specs=[vmem],
        out_specs=vmem,
        out_shape=jax.ShapeDtypeStruct((2 * bands, 3, row_count, cols), jnp.bfloat16),
        compiler_params=roomy,
    )(arrived)
    handled, first, lone, whole = lax.optimization_barrier((handled, first, lone, whole))
    first = [jnp.transpose(array, (0, 2, 1, 3)) for array in first]
    lone = [jnp.transpose(array, (1, 0, 2)) for array in lone]
    whole = [jnp.transpose(array, (0, 2, 1, 3)) for array in whole]
    fields = lax.all_to_all(handled, ("lat", "lev"), 0, 0, tiled=True)

    handling = lax.dynamic_index_in_dim(
        jnp.array(order, jnp.int32).reshape(2 * bands, 3), 2 * lat + lev, 0, keepdims=False
    )
    parity = jnp.take(wave_list, handling, mode="clip") % 2
    coefficients = pl.pallas_call(
        transform_kernel,
        in_specs=[smem] + [any_space] * 12,
        out_specs=vmem,
        out_shape=jax.ShapeDtypeStruct((2 * bands, 3, 2, width // 2, cols), jnp.bfloat16),
        scratch_shapes=[
            pltpu.VMEM((3, 2, bands * rows, 2 * cols), jnp.bfloat16),
            pltpu.VMEM((3, 2, bands * rows, reach), jnp.bfloat16),
            pltpu.VMEM((2 * bands, 3, row_count, cols), jnp.bfloat16),
            pltpu.SemaphoreType.DMA((12,)),
        ],
        compiler_params=pltpu.CompilerParams(vmem_limit_bytes=60 * 1024 * 1024),
    )(jnp.concatenate([place, parity]), *first, *lone, *whole, fields)

    owned = lax.all_to_all(coefficients, ("lat", "lev"), 0, 0, tiled=True)
    piece = width // 2
    lowest = wave_list * stride + wave_list % 2 * (stride - 1)
    lowest = jnp.broadcast_to(lowest[:, None], (slot_count, cols))
    return pl.pallas_call(
        spread_kernel,
        in_specs=[smem, vmem, vmem],
        out_specs=vmem,
        out_shape=jax.ShapeDtypeStruct((2, piece, 2, slot_count, cols), jnp.bfloat16),
        compiler_params=roomy,
    )(place, lowest, owned)


def solution(mesh):
    placed = (P("wave", "lat", "lev"), P("wave", "lat", None, "lev"), P("wave"))
    return jax.shard_map(
        shards,
        mesh=mesh,
        in_specs=placed,
        out_specs=P(None, "lat", None, "wave", "lev"),
        check_vma=False,
    )
```

time: 422 us -> 193 us (0.46)
  blocking collectives: 94.4 us -> 0 us
  waiting for transfers between devices: 193 us -> 98.9 us
  local copies, waits for them, and re-layouts: 68 us -> 26 us
  starting transfers between devices: 19.4 us -> 50.4 us
  matrix products: 18.1 us -> 0 us
  Pallas kernels: 0 us -> 15.7 us
  between operations: 14.2 us -> 0.22 us
  other arithmetic: 13.3 us -> 0.73 us
    unnamed x3 -> x0, waiting for transfers between devices: 91.1 us -> none
    all_to_all x0 -> x4, waiting for transfers between devices: none -> 57.2 us  [the longest x1 35.7 us: shards(): fields = lax.all_to_all(handled, ('lat', 'lev'), 0, 0, tiled=True)]
    unnamed x1 -> x0, blocking collectives: 56.7 us -> none
    all_gather x1 -> x0, waiting for transfers between devices: 54.2 us -> none  [shards(): whole_table = lax.all_gather(legendre, 'lev', axis=3, tiled=True)]
    all_to_all x1 -> x0, blocking collectives: 37.7 us -> none  [shards(): lax.all_to_all(outgoing, 'wave', split_axis=0, concat_axis=0, tiled=True)]
    all_to_all x0 -> x4, starting transfers between devices: none -> 29.5 us  [the longest x1 10 us: shards(): lax.all_to_all(listing.reshape(blocks, -1), 'wave', 0, 0, tiled=True)]
    another operation x3 -> x0, local copies, waits for them, and re-layouts: 25.1 us -> none  [the longest x2 25 us: degree_terms(): return jnp.stack(results, axis=1)]
    unnamed x15 -> x26, local copies, waits for them, and re-layouts: 29.7 us -> 10.9 us
  transfers between devices with their start and end apart: 5 -> 16, of which waited for: 5 -> 7; matrix products, arithmetic and copies ran while one was open for 4% -> 6% of each run, Pallas kernels for 0% -> 2%
where the time goes in v1:
time: 193 us; the launch traced here: 192 us
  waiting for transfers between devices  98.9 us (51%)
  starting transfers between devices  50.4 us (26%)
  local copies, waits for them, and re-layouts  26 us (13%)
  Pallas kernels  15.7 us (8%)
    ppermute x10, waiting for transfers between devices, hopped(): return lax.ppermute(array, 'lat', [(i, i ^ hop) for i in range(bands)])  40.2 us
    all_to_all x1, waiting for transfers between devices, shards(): fields = lax.all_to_all(handled, ('lat', 'lev'), 0, 0, tiled=True)  35.7 us
    all_to_all x1, waiting for transfers between devices, shards(): owned = lax.all_to_all(coefficients, ('lat', 'lev'), 0, 0, tiled=True)  21.3 us
    ppermute x10, starting transfers between devices, hopped(): return lax.ppermute(array, 'lat', [(i, i ^ hop) for i in range(bands)])  18.3 us
    unnamed x26, local copies, waits for them, and re-layouts  10.9 us
    all_to_all x1, starting transfers between devices, shards(): lax.all_to_all(listing.reshape(blocks, -1), 'wave', 0, 0, tiled=True)  10 us
    all_to_all x1, starting transfers between devices, shards(): arrived = lax.all_to_all(outgoing, 'wave', 0, 0, tiled=True)  8.53 us
    pallas_call x1, Pallas kernels, shards(): pl.pallas_call(transform_kernel, in_specs=[smem] + [any_space] * 12, out_...  7.45 us
  transfers between devices with their start and end apart: 16, of which 7 were waited for; matrix products, arithmetic and copies ran while one was open for 6% of the time, Pallas kernels for 2%

profile of v1, /device:TPU:1, one launch (start us, length us, event | category | flops | bytes accessed | tf_op | source)
XLA Modules:
  0.0 192.0 jit_solution(11917337996970862181)
XLA Ops:
  0.0 2.4 %slice.6 = bf16[4,128,2,256]{3,2,1,0:T(2,128)(2,1)} slice(bf16[32,128,2,512]{3,2,1,0:T(2,128)(2,1)} %table.1), slice={[24:28], [0:128], [0:2], [256:512]} | slice | bytes 1048576 | tf_op jit(solution)/shard_map/slice | solution.py:157
  2.4 1.1 slice.7
  3.5 1.3 collective-permute-start
  4.8 1.3 all_to_all.15
  6.1 10.0 %all-to-all-start = ((s32[16,1,2]{2,1,0:T(1,128)}), s32[16,1,2]{2,1,0:T(1,128)S(1)}, u32[]{:S(2)}, u32[]{:S(2)}) async-start(s32[16,1,2]{2,1,0:T(1,128)} %bitcast.3), calls=%async_computation | async-start | bytes 16384 | tf_op jit(solution)/shard_map/all_to_all | solution.py:163
  16.2 1.3 collective-permute-start.1
  17.5 0.1 pad_add_fusion.place
  17.6 3.4 %copy-done.1 = bf16[32,128,2,512]{3,2,1,0:T(2,128)(2,1)S(1)} copy-done((bf16[32,128,2,512]{3,2,1,0:T(2,128)(2,1)S(1)}, bf16[32,128,2,512]{3,2,1,0:T(2,128)(2,1)}, u32[]{:S(2)}) %copy-start.1) | copy-done | bytes 8388632
  21.0 0.6 shard_map.46
  21.6 0.8 copy-done.4
  22.4 0.8 copy-done.6
  23.2 0.2 all-to-all-done
  23.5 0.1 reshape.34
  23.6 2.1 %gather_fusion.1 = bf16[32,256,128]{2,1,0:T(8,128)(2,1)} fusion(bf16[32,256,128]{2,1,0:T(8,128)(2,1)S(1)} %copy-done, s32[1024]{0:T(1024)S(1)} %pad_clamp_fusion), kind=kCustom, calls=%fused_computation.1 | custom fusion | bytes 4194432 | tf_op jit(solution)/shard_map/jit(_take)/gather | solution.py:165
  25.7 1.6 collective-permute-done.1.slim
  27.3 0.0 collective-permute-done.wide
  27.3 8.5 %all-to-all-start.1 = ((bf16[32,256,128]{2,1,0:T(8,128)(2,1)}), bf16[32,256,128]{2,1,0:T(8,128)(2,1)}, u32[]{:S(2)}, u32[]{:S(2)}) async-start(bf16[32,256,128]{2,1,0:T(8,128)(2,1)} %gather_fusion.1), calls=%async_computation.1 | async-start | bytes 4194304 | tf_op jit(solution)/shard_map/all_to_all | solution.py:176
  35.8 1.1 copy.28
  36.9 1.4 collective-permute-start.2
  38.3 0.1 copy.29
  38.4 2.0 %collective-permute-start.3 = (bf16[2,128,2,512]{3,1,2,0:T(8,128)(2,1)S(1)}, bf16[2,128,2,512]{3,1,2,0:T(8,128)(2,1)S(1)}, u32[]{:S(2)}, u32[]{:S(2)}) collective-permute-start(bf16[2,128,2,512]{3,1,2,0:T(8,128)(2,1)S(1)} %copy.29), channel_id=1, source_target_pairs={{0,192},{32,224},{64,128},{96,160},{128,64},{160,96},{192,0},{224,... | collective-permute-start | bytes 1572872 | tf_op jit(solution)/shard_map/ppermute | solution.py:152
  40.4 3.4 %copy-done.2 = bf16[32,128,2,512]{3,2,1,0:T(2,128)(2,1)S(1)} copy-done((bf16[32,128,2,512]{3,2,1,0:T(2,128)(2,1)S(1)}, bf16[32,128,2,512]{3,2,1,0:T(2,128)(2,1)}, u32[]{:S(2)}) %copy-start.2) | copy-done | bytes 8388632
  43.7 1.9 shard_map.47
  45.6 0.1 copy.31
  45.7 2.8 %collective-permute-start.5 = (bf16[3,128,2,512]{3,1,2,0:T(8,128)(2,1)S(1)}, bf16[3,128,2,512]{3,1,2,0:T(8,128)(2,1)S(1)}, u32[]{:S(2)}, u32[]{:S(2)}) collective-permute-start(bf16[3,128,2,512]{3,1,2,0:T(8,128)(2,1)S(1)} %copy.31), channel_id=1, source_target_pairs={{0,96},{32,64},{64,32},{96,0},{128,224},{160,192},{192,160},{224,1... | collective-permute-start | bytes 2359304 | tf_op jit(solution)/shard_map/ppermute | solution.py:152
  48.5 0.1 copy.32
  48.6 0.5 collective-permute-start.6
  49.1 0.1 copy.30
  49.1 1.5 collective-permute-start.4
  50.6 1.0 copy.36
  51.6 1.0 copy.37
  52.6 0.0 collective-permute-done.2
  52.6 3.9 %collective-permute-start.10 = (bf16[3,128,2,512]{3,1,2,0:T(8,128)(2,1)}, bf16[3,128,2,512]{3,1,2,0:T(8,128)(2,1)}, u32[]{:S(2)}, u32[]{:S(2)}) collective-permute-start(bf16[3,128,2,512]{3,1,2,0:T(8,128)(2,1)} %copy.36), channel_id=1, source_target_pairs={{0,160},{32,128},{64,224},{96,192},{128,32},{160,0},{192,96},{224,... | collective-permute-start | bytes 2359304 | tf_op jit(solution)/shard_map/ppermute | solution.py:152
  56.5 0.0 collective-permute-done.3
  56.5 0.0 collective-permute-start.11
  56.5 0.8 copy.33
  57.3 0.7 copy.34
  58.0 0.7 copy.35
  58.8 20.8 %collective-permute-done.4 = bf16[2,128,2,512]{3,1,2,0:T(8,128)(2,1)S(1)} collective-permute-done((bf16[2,128,2,512]{3,1,2,0:T(8,128)(2,1)S(1)}, bf16[2,128,2,512]{3,1,2,0:T(8,128)(2,1)S(1)}, u32[]{:S(2)}, u32[]{:S(2)}) %collective-permute-start.4) | collective-permute-done | bytes 524320 | tf_op jit(solution)/shard_map/ppermute | solution.py:152
  79.6 0.0 collective-permute-start.7
  79.6 0.0 collective-permute-done.5
  79.6 2.0 %collective-permute-start.8 = (bf16[128,2,512]{2,0,1:T(8,128)(2,1)}, bf16[128,2,512]{2,0,1:T(8,128)(2,1)}, u32[]{:S(2)}, u32[]{:S(2)}) collective-permute-start(bf16[128,2,512]{2,0,1:T(8,128)(2,1)} %copy.34), channel_id=1, source_target_pairs={{0,192},{32,224},{64,128},{96,160},{128,64},{160,96},{192,0},{224,... | collective-permute-start | bytes 786440 | tf_op jit(solution)/shard_map/ppermute | solution.py:152
  81.6 14.8 %collective-permute-done.6 = bf16[3,128,2,512]{3,1,2,0:T(8,128)(2,1)S(1)} collective-permute-done((bf16[3,128,2,512]{3,1,2,0:T(8,128)(2,1)S(1)}, bf16[3,128,2,512]{3,1,2,0:T(8,128)(2,1)S(1)}, u32[]{:S(2)}, u32[]{:S(2)}) %collective-permute-start.6) | collective-permute-done | bytes 786464 | tf_op jit(solution)/shard_map/ppermute | solution.py:152
  96.5 0.9 copy-done.9
  97.4 4.3 %collective-permute-start.9 = (bf16[128,2,512]{2,0,1:T(8,128)(2,1)}, bf16[128,2,512]{2,0,1:T(8,128)(2,1)}, u32[]{:S(2)}, u32[]{:S(2)}) collective-permute-start(bf16[128,2,512]{2,0,1:T(8,128)(2,1)} %copy.35), channel_id=1, source_target_pairs={{0,128},{32,160},{64,192},{96,224},{128,0},{160,32},{192,64},{224,... | collective-permute-start | bytes 786440 | tf_op jit(solution)/shard_map/ppermute | solution.py:152
  101.7 0.0 all-to-all-done.1.arrived
  101.7 1.9 %shard_map.48 = bf16[16,3,256,128]{3,2,1,0:T(8,128)(2,1)S(1)} custom-call(bf16[32,256,128]{2,1,0:T(8,128)(2,1)} %all-to-all-done.1.arrived), custom_call_target="tpu_custom_call" | custom-call | tf_op jit(solution)/shard_map/pallas_call | solution.py:193
  103.6 1.7 copy-done.3
  105.3 0.0 collective-permute-done.7
  105.3 4.5 %collective-permute-done.8 = bf16[128,2,512]{2,0,1:T(8,128)(2,1)} collective-permute-done((bf16[128,2,512]{2,0,1:T(8,128)(2,1)}, bf16[128,2,512]{2,0,1:T(8,128)(2,1)}, u32[]{:S(2)}, u32[]{:S(2)}) %collective-permute-start.8) | collective-permute-done | bytes 262176 | tf_op jit(solution)/shard_map/ppermute | solution.py:152
  109.8 0.0 collective-permute-done.9
  109.9 0.0 collective-permute-done.10
  109.9 0.0 collective-permute-done.11
  109.9 5.8 %all-to-all-start.2 = ((bf16[16,3,256,128]{3,2,1,0:T(8,128)(2,1)}), bf16[16,3,256,128]{3,2,1,0:T(8,128)(2,1)}, u32[]{:S(2)}, u32[]{:S(2)}) async-start(bf16[16,3,256,128]{3,2,1,0:T(8,128)(2,1)} %copy-done.3), calls=%async_computation.2 | async-start | bytes 6291456 | tf_op jit(solution)/shard_map/all_to_all | solution.py:204
  115.7 0.7 dynamic-slice_bitcast_fusion
  116.4 0.6 gather_fusion
  117.1 0.6 pad_add_fusion.1.place
  117.6 1.0 copy.40
  118.6 35.7 %all-to-all-done.2.refs_11_ = bf16[16,3,256,128]{3,2,1,0:T(8,128)(2,1)} async-done(((bf16[16,3,256,128]{3,2,1,0:T(8,128)(2,1)}), bf16[16,3,256,128]{3,2,1,0:T(8,128)(2,1)}, u32[]{:S(2)}, u32[]{:S(2)}) %all-to-all-start.2) | async-done | bytes 3145760 | tf_op jit(solution)/shard_map/all_to_all | solution.py:204
  154.3 7.4 %shard_map.49 = bf16[16,3,2,64,128]{4,3,2,1,0:T(8,128)(2,1)} custom-call(s32[5]{0:T(128)} %pad_add_fusion.1.place, bf16[2,2,128,512]{3,2,1,0:T(8,128)(2,1)} %bitcast.21, bf16[2,2,128,512]{3,2,1,0:T(8,128)(2,1)} %bitcast.22, bf16[2,2,128,512]{3,2,1,0:T(8,128)(2,1)} %bitcast.23, bf16[2,128,512]{2,1,0:T(8,128)(2,1)} %bitcast.7.refs_3_, ...), custom_call_target="tpu_custom_call" | custom-call | tf_op jit(solution)/shard_map/pallas_call | solution.py:210
  161.8 5.1 %all-to-all-start.3 = ((bf16[16,3,2,64,128]{4,3,2,1,0:T(8,128)(2,1)}), bf16[16,3,2,64,128]{4,3,2,1,0:T(8,128)(2,1)}, u32[]{:S(2)}, u32[]{:S(2)}) async-start(bf16[16,3,2,64,128]{4,3,2,1,0:T(8,128)(2,1)} %shard_map.49), calls=%async_computation.3 | async-start | bytes 3145728 | tf_op jit(solution)/shard_map/all_to_all | solution.py:224
  166.9 21.3 %all-to-all-done.3.owned = bf16[16,3,2,64,128]{4,3,2,1,0:T(8,128)(2,1)} async-done(((bf16[16,3,2,64,128]{4,3,2,1,0:T(8,128)(2,1)}), bf16[16,3,2,64,128]{4,3,2,1,0:T(8,128)(2,1)}, u32[]{:S(2)}, u32[]{:S(2)}) %all-to-all-start.3) | async-done | bytes 1572896 | tf_op jit(solution)/shard_map/all_to_all | solution.py:224
  188.1 0.1 broadcast_in_dim.12.lowest
  188.2 3.8 %shard_map.50 = bf16[2,64,2,32,128]{4,3,2,1,0:T(8,128)(2,1)} custom-call(s32[2]{0:T(128)S(1)} %pad_add_fusion.place, s32[32,128]{1,0:T(8,128)S(1)} %broadcast_in_dim.12.lowest, bf16[16,3,2,64,128]{4,3,2,1,0:T(8,128)(2,1)} %all-to-all-done.3.owned), custom_call_target="tpu_custom_call" | custom-call | tf_op jit(solution)/shard_map/pallas_call | solution.py:228
  (25 shorter events, 0.1 us)
Async XLA Ops:
  0.0 23.6 %copy-start = (bf16[32,256,128]{2,1,0:T(8,128)(2,1)S(1)}, bf16[32,256,128]{2,1,0:T(8,128)(2,1)}, u32[]{:S(2)}) copy-start(bf16[32,256,128]{2,1,0:T(8,128)(2,1)} %param.4) | copy-start | bytes 6291460
  3.5 23.8 %collective-permute-start = (bf16[4,128,2,256]{3,2,1,0:T(2,128)(2,1)}, bf16[4,128,2,256]{3,2,1,0:T(2,128)(2,1)S(1)}, u32[]{:S(2)}, u32[]{:S(2)}) collective-permute-start(bf16[4,128,2,256]{3,2,1,0:T(2,128)(2,1)} %slice.6), channel_id=1, source_target_pairs={{1,0},{3,2},{5,4},{7,6},{9,8},{11,10},{13,12},{15,14},{17,16},{19,... | collective-permute-start | bytes 1572872 | tf_op jit(solution)/shard_map/ppermute | solution.py:160
  6.1 17.3 %all-to-all-start = ((s32[16,1,2]{2,1,0:T(1,128)}), s32[16,1,2]{2,1,0:T(1,128)S(1)}, u32[]{:S(2)}, u32[]{:S(2)}) async-start(s32[16,1,2]{2,1,0:T(1,128)} %bitcast.3), calls=%async_computation | async-start | bytes 16384 | tf_op jit(solution)/shard_map/all_to_all | solution.py:163
  16.2 11.1 %collective-permute-start.1 = (bf16[4,128,2,128]{3,2,1,0:T(2,128)(2,1)S(1)}, bf16[4,128,2,128]{3,2,1,0:T(2,128)(2,1)}, u32[]{:S(2)}, u32[]{:S(2)}) collective-permute-start(bf16[4,128,2,128]{3,2,1,0:T(2,128)(2,1)S(1)} %slice.7), channel_id=1, source_target_pairs={{1,0},{3,2},{5,4},{7,6},{9,8},{11,10},{13,12},{15,14},{17,16},{19,... | collective-permute-start | bytes 786440 | tf_op jit(solution)/shard_map/ppermute | solution.py:161
  17.6 3.4 %copy-start.1 = (bf16[32,128,2,512]{3,2,1,0:T(2,128)(2,1)S(1)}, bf16[32,128,2,512]{3,2,1,0:T(2,128)(2,1)}, u32[]{:S(2)}) copy-start(bf16[32,128,2,512]{3,2,1,0:T(2,128)(2,1)} %table.1) | copy-start | bytes 25165828
  21.6 0.8 copy-start.4
  22.4 0.8 copy-start.6
  27.3 74.4 %all-to-all-start.1 = ((bf16[32,256,128]{2,1,0:T(8,128)(2,1)}), bf16[32,256,128]{2,1,0:T(8,128)(2,1)}, u32[]{:S(2)}, u32[]{:S(2)}) async-start(bf16[32,256,128]{2,1,0:T(8,128)(2,1)} %gather_fusion.1), calls=%async_computation.1 | async-start | bytes 4194304 | tf_op jit(solution)/shard_map/all_to_all | solution.py:176
  36.9 15.7 %collective-permute-start.2 = (bf16[2,128,2,512]{3,1,2,0:T(8,128)(2,1)S(1)}, bf16[2,128,2,512]{3,1,2,0:T(8,128)(2,1)S(1)}, u32[]{:S(2)}, u32[]{:S(2)}) collective-permute-start(bf16[2,128,2,512]{3,1,2,0:T(8,128)(2,1)S(1)} %copy.28), channel_id=1, source_target_pairs={{0,64},{32,96},{64,0},{96,32},{128,192},{160,224},{192,128},{224,1... | collective-permute-start | bytes 1572872 | tf_op jit(solution)/shard_map/ppermute | solution.py:152
  38.4 18.1 %collective-permute-start.3 = (bf16[2,128,2,512]{3,1,2,0:T(8,128)(2,1)S(1)}, bf16[2,128,2,512]{3,1,2,0:T(8,128)(2,1)S(1)}, u32[]{:S(2)}, u32[]{:S(2)}) collective-permute-start(bf16[2,128,2,512]{3,1,2,0:T(8,128)(2,1)S(1)} %copy.29), channel_id=1, source_target_pairs={{0,192},{32,224},{64,128},{96,160},{128,64},{160,96},{192,0},{224,... | collective-permute-start | bytes 1572872 | tf_op jit(solution)/shard_map/ppermute | solution.py:152
  40.4 3.4 %copy-start.2 = (bf16[32,128,2,512]{3,2,1,0:T(2,128)(2,1)S(1)}, bf16[32,128,2,512]{3,2,1,0:T(2,128)(2,1)}, u32[]{:S(2)}) copy-start(bf16[32,128,2,512]{3,2,1,0:T(2,128)(2,1)} %table.1) | copy-start | bytes 25165828
  45.6 3.4 %copy-start.5 = (bf16[2,128,2,512]{3,2,1,0:T(2,128)(2,1)S(1)}, bf16[2,128,2,512]{3,2,1,0:T(2,128)(2,1)}, u32[]{:S(2)}) copy-start(bf16[2,128,2,512]{3,2,1,0:T(2,128)(2,1)} %copy-done.4) | copy-start | bytes 1572868
  45.7 33.9 %collective-permute-start.5 = (bf16[3,128,2,512]{3,1,2,0:T(8,128)(2,1)S(1)}, bf16[3,128,2,512]{3,1,2,0:T(8,128)(2,1)S(1)}, u32[]{:S(2)}, u32[]{:S(2)}) collective-permute-start(bf16[3,128,2,512]{3,1,2,0:T(8,128)(2,1)S(1)} %copy.31), channel_id=1, source_target_pairs={{0,96},{32,64},{64,32},{96,0},{128,224},{160,192},{192,160},{224,1... | collective-permute-start | bytes 2359304 | tf_op jit(solution)/shard_map/ppermute | solution.py:152
  48.6 47.9 %collective-permute-start.6 = (bf16[3,128,2,512]{3,1,2,0:T(8,128)(2,1)S(1)}, bf16[3,128,2,512]{3,1,2,0:T(8,128)(2,1)S(1)}, u32[]{:S(2)}, u32[]{:S(2)}) collective-permute-start(bf16[3,128,2,512]{3,1,2,0:T(8,128)(2,1)S(1)} %copy.32), channel_id=1, source_target_pairs={{0,224},{32,192},{64,160},{96,128},{128,96},{160,64},{192,32},{224... | collective-permute-start | bytes 2359304 | tf_op jit(solution)/shard_map/ppermute | solution.py:152
  49.1 30.5 %collective-permute-start.4 = (bf16[2,128,2,512]{3,1,2,0:T(8,128)(2,1)S(1)}, bf16[2,128,2,512]{3,1,2,0:T(8,128)(2,1)S(1)}, u32[]{:S(2)}, u32[]{:S(2)}) collective-permute-start(bf16[2,128,2,512]{3,1,2,0:T(8,128)(2,1)S(1)} %copy.30), channel_id=1, source_target_pairs={{0,128},{32,160},{64,192},{96,224},{128,0},{160,32},{192,64},{224,... | collective-permute-start | bytes 1572872 | tf_op jit(solution)/shard_map/ppermute | solution.py:152
  52.6 43.9 %copy-start.10 = (bf16[2,128,2,512]{3,1,2,0:T(8,128)(2,1)}, bf16[2,128,2,512]{3,1,2,0:T(8,128)(2,1)S(1)}, u32[]{:S(2)}) copy-start(bf16[2,128,2,512]{3,1,2,0:T(8,128)(2,1)S(1)} %collective-permute-done.2) | copy-start | bytes 1572868
  52.6 57.3 %collective-permute-start.10 = (bf16[3,128,2,512]{3,1,2,0:T(8,128)(2,1)}, bf16[3,128,2,512]{3,1,2,0:T(8,128)(2,1)}, u32[]{:S(2)}, u32[]{:S(2)}) collective-permute-start(bf16[3,128,2,512]{3,1,2,0:T(8,128)(2,1)} %copy.36), channel_id=1, source_target_pairs={{0,160},{32,128},{64,224},{96,192},{128,32},{160,0},{192,96},{224,... | collective-permute-start | bytes 2359304 | tf_op jit(solution)/shard_map/ppermute | solution.py:152
  56.5 39.9 %copy-start.11 = (bf16[2,128,2,512]{3,1,2,0:T(8,128)(2,1)}, bf16[2,128,2,512]{3,1,2,0:T(8,128)(2,1)S(1)}, u32[]{:S(2)}) copy-start(bf16[2,128,2,512]{3,1,2,0:T(8,128)(2,1)S(1)} %collective-permute-done.3) | copy-start | bytes 1572868
  56.5 53.4 %collective-permute-start.11 = (bf16[3,128,2,512]{3,1,2,0:T(8,128)(2,1)}, bf16[3,128,2,512]{3,1,2,0:T(8,128)(2,1)}, u32[]{:S(2)}, u32[]{:S(2)}) collective-permute-start(bf16[3,128,2,512]{3,1,2,0:T(8,128)(2,1)} %copy.37), channel_id=1, source_target_pairs={{0,32},{32,0},{64,96},{96,64},{128,160},{160,128},{192,224},{224,1... | collective-permute-start | bytes 2359304 | tf_op jit(solution)/shard_map/ppermute | solution.py:152
  79.6 39.0 %copy-start.12 = (bf16[2,128,2,512]{3,1,2,0:T(8,128)(2,1)}, bf16[2,128,2,512]{3,1,2,0:T(8,128)(2,1)S(1)}, u32[]{:S(2)}) copy-start(bf16[2,128,2,512]{3,1,2,0:T(8,128)(2,1)S(1)} %collective-permute-done.4) | copy-start | bytes 1572868
  79.6 25.7 %collective-permute-start.7 = (bf16[128,2,512]{2,0,1:T(8,128)(2,1)}, bf16[128,2,512]{2,0,1:T(8,128)(2,1)}, u32[]{:S(2)}, u32[]{:S(2)}) collective-permute-start(bf16[128,2,512]{2,0,1:T(8,128)(2,1)} %copy.33), channel_id=1, source_target_pairs={{0,64},{32,96},{64,0},{96,32},{128,192},{160,224},{192,128},{224,1... | collective-permute-start | bytes 786440 | tf_op jit(solution)/shard_map/ppermute | solution.py:152
  79.6 16.8 %copy-start.8 = (bf16[3,128,2,512]{3,1,2,0:T(8,128)(2,1)}, bf16[3,128,2,512]{3,1,2,0:T(8,128)(2,1)S(1)}, u32[]{:S(2)}) copy-start(bf16[3,128,2,512]{3,1,2,0:T(8,128)(2,1)S(1)} %collective-permute-done.5) | copy-start | bytes 2359300
  79.6 30.2 %collective-permute-start.8 = (bf16[128,2,512]{2,0,1:T(8,128)(2,1)}, bf16[128,2,512]{2,0,1:T(8,128)(2,1)}, u32[]{:S(2)}, u32[]{:S(2)}) collective-permute-start(bf16[128,2,512]{2,0,1:T(8,128)(2,1)} %copy.34), channel_id=1, source_target_pairs={{0,192},{32,224},{64,128},{96,160},{128,64},{160,96},{192,0},{224,... | collective-permute-start | bytes 786440 | tf_op jit(solution)/shard_map/ppermute | solution.py:152
  96.5 0.9 copy-start.9
  97.4 12.5 %collective-permute-start.9 = (bf16[128,2,512]{2,0,1:T(8,128)(2,1)}, bf16[128,2,512]{2,0,1:T(8,128)(2,1)}, u32[]{:S(2)}, u32[]{:S(2)}) collective-permute-start(bf16[128,2,512]{2,0,1:T(8,128)(2,1)} %copy.35), channel_id=1, source_target_pairs={{0,128},{32,160},{64,192},{96,224},{128,0},{160,32},{192,64},{224,... | collective-permute-start | bytes 786440 | tf_op jit(solution)/shard_map/ppermute | solution.py:152
  103.6 1.7 copy-start.3
  105.3 11.1 %copy-start.7 = (s32[32]{0:T(128)S(1)}, s32[32]{0:T(128)}, u32[]{:S(2)}) copy-start(s32[32]{0:T(128)} %param.6) | copy-start | bytes 388
  109.9 44.4 %all-to-all-start.2 = ((bf16[16,3,256,128]{3,2,1,0:T(8,128)(2,1)}), bf16[16,3,256,128]{3,2,1,0:T(8,128)(2,1)}, u32[]{:S(2)}, u32[]{:S(2)}) async-start(bf16[16,3,256,128]{3,2,1,0:T(8,128)(2,1)} %copy-done.3), calls=%async_computation.2 | async-start | bytes 6291456 | tf_op jit(solution)/shard_map/all_to_all | solution.py:204
  161.8 26.4 %all-to-all-start.3 = ((bf16[16,3,2,64,128]{4,3,2,1,0:T(8,128)(2,1)}), bf16[16,3,2,64,128]{4,3,2,1,0:T(8,128)(2,1)}, u32[]{:S(2)}, u32[]{:S(2)}) async-start(bf16[16,3,2,64,128]{4,3,2,1,0:T(8,128)(2,1)} %shard_map.49), calls=%async_computation.3 | async-start | bytes 3145728 | tf_op jit(solution)/shard_map/all_to_all | solution.py:224

commit v2 on v1

v2 whole, which is shorter than its diff:
```python
import functools

import jax
import jax.numpy as jnp
from jax import lax
from jax.experimental import pallas as pl
from jax.experimental.pallas import tpu as pltpu
from jax.sharding import PartitionSpec as P

NN = 2048
FIRST = (2, 6, 4)
LAST = (3, 7, 5, 1)


def band_to(lat, hop):
    if hop in (2, 3):
        return lat ^ (hop + 4 * (lat % 2))
    if hop in (6, 7):
        return lat ^ (hop - 4 * (lat % 2))
    return lat ^ hop


def band_from(lat, hop):
    if hop == 3:
        return lat ^ (7 - 4 * (lat % 2))
    if hop == 7:
        return lat ^ (3 + 4 * (lat % 2))
    return band_to(lat, hop)


def after(first, *arrays):
    return lax.optimization_barrier((first, *arrays))[1:]


def first_kernel(place, table, *refs):
    outs, cross, sems = refs[:3], *refs[3:]
    reach, cut = table.shape[3], cross.shape[3]
    copies = [
        pltpu.make_async_copy(table.at[24:28, :, :, reach - cut : reach], cross.at[0:4], sems.at[6])
    ]
    for n in range(4):
        lanes = slice(n % 2 * cut // 2, (n % 2 + 1) * cut // 2)
        copies.append(
            pltpu.make_async_copy(
                table.at[28 + n, :, :, reach - cut // 2 : reach],
                cross.at[4 + n // 2, :, :, lanes],
                sems.at[7 + n],
            )
        )
    for n, hop in enumerate(FIRST):
        band = band_to(place[0], hop)
        copies += [
            pltpu.make_async_copy(table.at[band], outs[n].at[0], sems.at[2 * n]),
            pltpu.make_async_copy(table.at[15 - band], outs[n].at[1], sems.at[2 * n + 1]),
        ]
    for copy in copies:
        copy.start()
    for copy in copies:
        copy.wait()


def rest_kernel(place, table, cross, *refs):
    outs, sems = refs[:8], refs[8]
    lat, lev = place[0], place[1]
    reach, cut = table.shape[3], cross.shape[3]
    end = cut // 2
    copies, lone = [], []
    for n, hop in enumerate((*FIRST, 0, *LAST)):
        band, out = band_to(lat, hop), outs[n]
        if n >= 3:
            copies += [
                pltpu.make_async_copy(table.at[band], out.at[0], sems.at[n, 0]),
                pltpu.make_async_copy(table.at[15 - band], out.at[1], sems.at[n, 1]),
            ]
            out = out.at[2]
        lone.append((band, out, pltpu.make_async_copy(table.at[16 + band], out, sems.at[n, 2])))
    for copy in copies:
        copy.start()

    @pl.when(lev == 0)
    def _():
        for band, out, _ in lone:
            out[:, :, 0 : reach - cut] = jnp.zeros_like(out[:, :, 0 : reach - cut])

            @pl.when(band < 4)
            def _():
                out[:, :, reach - cut :] = cross[band]

            @pl.when(band >= 4)
            def _():
                lanes = pl.ds(pl.multiple_of(band % 2 * end, end), end)
                out[:, :, reach - cut : reach - end] = jnp.zeros_like(out[:, :, 0:end])
                out[:, :, reach - end :] = cross[2 + band // 2, :, :, lanes]

    @pl.when(lev != 0)
    def _():
        for _, _, copy in lone:
            copy.start()
        for _, _, copy in lone:
            copy.wait()

    for copy in copies:
        copy.wait()


def pack_kernel(*refs):
    first, lone, whole, out = refs[:3], refs[3:6], refs[6:11], refs[11]
    rows = lone[0].shape[0]
    for n, hop in enumerate((*FIRST, 0, *LAST)):
        for f in range(3):
            if n >= 3:
                values = whole[n - 3][f]
            else:
                values = first[n][f] if f < 2 else lone[n][...]
            out[f, :, hop * rows : (hop + 1) * rows, :] = jnp.swapaxes(values, 0, 1)


def transform_kernel(place, *refs):
    packed, arrived, out, source, table, fields, sems = refs
    lat = place[0]
    rows, reach = table.shape[2] // 8, table.shape[3]
    width = reach // 4
    half = width // 2
    cols = arrived.shape[3]
    fetch = pltpu.make_async_copy(arrived, fields, sems.at[0])
    fetch.start()
    load = pltpu.make_async_copy(packed, table, sems.at[1])
    load.start()
    at_row = lax.broadcasted_iota(jnp.int32, (rows, rows), 0)
    at_col = lax.broadcasted_iota(jnp.int32, (rows, rows), 1)
    flip = (at_row + at_col == rows - 1).astype(jnp.bfloat16)
    fetch.wait()
    pairs = [(f, v) for f in range(3) for v in range(2)]
    for hop in range(8):
        band = band_from(lat, hop)
        near = [fields[2 * band + v, f, 0:rows, :] for f, v in pairs]
        far = [fields[2 * (7 - band) + v, f, rows : 2 * rows, :] for f, v in pairs]
        mirrored = jnp.dot(flip, jnp.concatenate(far, 1), preferred_element_type=jnp.float32)
        for n, (f, v) in enumerate(pairs):
            one = near[n].astype(jnp.float32)
            other = mirrored[:, n * cols : (n + 1) * cols]
            odd = place[2 + f] == 1
            other = jnp.where(odd, -other, other)
            here = (slice(hop * rows, (hop + 1) * rows), slice(v * cols, (v + 1) * cols))
            source[f, 0, *here] = (one + other).astype(jnp.bfloat16)
            source[f, 1, *here] = (one - other).astype(jnp.bfloat16)
    load.wait()
    for f in range(3):
        for p in range(2):
            for n in range(4):
                values = lax.dot_general(
                    table[f, p, :, n * width : (n + 1) * width],
                    source[f, p],
                    (((0,), (0,)), ((), ())),
                    preferred_element_type=jnp.float32,
                ).astype(jnp.bfloat16)
                for h in range(2):
                    for v in range(2):
                        out[2 * (2 * n + h) + v, f, p] = values[
                            h * half : (h + 1) * half, v * cols : (v + 1) * cols
                        ]


def pick_kernel(order, arrived, out):
    for n, slot in enumerate(order):
        out[n // 3, n % 3] = arrived[slot]


def spread_kernel(place, lowest, owned, out):
    piece, slots, cols = out.shape[1], out.shape[3], out.shape[4]
    bands = slots // 4
    up = range(bands)
    down = range(bands - 1, -1, -1)
    whole = [
        [(2 * m, 0) for m in up] + [(2 * m, 1) for m in down],
        [(2 * m + 1, 0) for m in up]
        + [(2 * m + 1, 1) for m in down]
        + [(2 * m + 1, 2) for m in up]
        + [(2 * m, 2) for m in up],
    ]
    for k in range(2):
        count = len(whole[k])
        q = lax.broadcasted_iota(jnp.int32, (piece, count, cols), 0) + (8 * k + place[0]) * piece
        for p in range(2):
            held = jnp.stack([owned[n, e, p].astype(jnp.float32) for n, e in whole[k]])
            held = jnp.transpose(held, (1, 0, 2))
            held = jnp.where(2 * q + p >= lowest[0:count][None], held, 0.0)
            out[k, :, p, 0:count] = held.astype(jnp.bfloat16)
            if count < slots:
                out[k, :, p, count:] = jnp.zeros((piece, slots - count, cols), jnp.bfloat16)


def shards(fourier, legendre, wave_list):
    roomy = pltpu.CompilerParams(vmem_limit_bytes=8 * 1024 * 1024)
    any_space = pl.BlockSpec(memory_space=pl.ANY)
    smem = pl.BlockSpec(memory_space=pltpu.SMEM)
    vmem = pl.BlockSpec(memory_space=pltpu.VMEM)
    lat, lev = lax.axis_index("lat"), lax.axis_index("lev")
    block_id = lax.axis_index("wave")
    slot_count, row_count, cols = fourier.shape
    bands, blocks = lax.axis_size("lat"), lax.axis_size("wave")
    rows, reach = legendre.shape[1], legendre.shape[3]
    width = reach // 4
    stride = NN // (slot_count * blocks)

    def hopped(array, hop):
        return lax.ppermute(array, "lat", [(i, band_to(i, hop)) for i in range(bands)])

    def shape_of(*dims):
        return jax.ShapeDtypeStruct(dims, jnp.bfloat16)

    place = jnp.stack([lat, lev]).astype(jnp.int32)
    full = pltpu.CompilerParams(vmem_limit_bytes=56 * 1024 * 1024)
    *first, cross = pl.pallas_call(
        first_kernel,
        in_specs=[smem, any_space],
        out_specs=[vmem] * 4,
        out_shape=[shape_of(2, rows, 2, reach)] * 3 + [shape_of(6, rows, 2, reach // 2)],
        scratch_shapes=[pltpu.SemaphoreType.DMA((11,))],
        compiler_params=full,
    )(place, legendre)
    cross, listing, *first = lax.optimization_barrier((cross, wave_list, *first))
    cross = lax.ppermute(cross, "lev", [(1, 0)])
    first = [hopped(array, hop) for array, hop in zip(first, FIRST)]

    wanted = lax.all_to_all(listing.reshape(blocks, -1), "wave", 0, 0, tiled=True)

    rest = pl.pallas_call(
        rest_kernel,
        in_specs=[smem, any_space, vmem],
        out_specs=[vmem] * 8,
        out_shape=[shape_of(rows, 2, reach)] * 3 + [shape_of(3, rows, 2, reach)] * 5,
        scratch_shapes=[pltpu.SemaphoreType.DMA((8, 3))],
        compiler_params=pltpu.CompilerParams(vmem_limit_bytes=52 * 1024 * 1024),
        cost_estimate=pl.CostEstimate(flops=10**9, bytes_accessed=2**20, transcendentals=0),
    )(place, legendre, cross)
    wanted, rest = lax.optimization_barrier((wanted, rest))
    local = (wanted - block_id * slot_count).reshape(-1)
    outgoing = jnp.take(fourier, local, axis=0, mode="clip")
    outgoing, first = lax.optimization_barrier((outgoing, first))
    arrived = lax.all_to_all(outgoing, "wave", 0, 0, tiled=True)
    lone, (mine, *whole) = rest[:3], rest[3:]
    whole = [mine] + [hopped(array, hop) for array, hop in zip(whole, LAST)]
    lone = [hopped(array, hop) for array, hop in zip(lone, FIRST)]

    order = []
    for m in range(bands):
        order += [m, 15 - m, 24 + m, m, 15 - m, 16 + m]
    handled = pl.pallas_call(
        functools.partial(pick_kernel, order),
        in_specs=[vmem],
        out_specs=vmem,
        out_shape=jax.ShapeDtypeStruct((2 * bands, 3, row_count, cols), jnp.bfloat16),
        compiler_params=roomy,
    )(arrived)
    handled, whole, lone = lax.optimization_barrier((handled, whole, lone))
    fields = lax.all_to_all(handled, ("lat", "lev"), 0, 0, tiled=True)

    packed = pl.pallas_call(
        pack_kernel,
        in_specs=[vmem] * 11,
        out_specs=vmem,
        out_shape=shape_of(3, 2, bands * rows, reach),
        compiler_params=roomy,
        cost_estimate=pl.CostEstimate(
            flops=2 * 10**10, bytes_accessed=24 * 1024 * 1024, transcendentals=0
        ),
    )(*first, *lone, *whole)

    handling = lax.dynamic_index_in_dim(
        jnp.array(order, jnp.int32).reshape(2 * bands, 3), 2 * lat + lev, 0, keepdims=False
    )
    parity = jnp.take(wave_list, handling, mode="clip") % 2
    coefficients = pl.pallas_call(
        transform_kernel,
        in_specs=[smem, any_space, any_space],
        out_specs=vmem,
        out_shape=jax.ShapeDtypeStruct((2 * bands, 3, 2, width // 2, cols), jnp.bfloat16),
        scratch_shapes=[
            pltpu.VMEM((3, 2, bands * rows, 2 * cols), jnp.bfloat16),
            pltpu.VMEM((3, 2, bands * rows, reach), jnp.bfloat16),
            pltpu.VMEM((2 * bands, 3, row_count, cols), jnp.bfloat16),
            pltpu.SemaphoreType.DMA((2,)),
        ],
        compiler_params=pltpu.CompilerParams(vmem_limit_bytes=60 * 1024 * 1024),
    )(jnp.concatenate([place, parity]), packed, fields)

    owned = lax.all_to_all(coefficients, ("lat", "lev"), 0, 0, tiled=True)
    piece = width // 2
    lowest = wave_list * stride + wave_list % 2 * (stride - 1)
    lowest = jnp.broadcast_to(lowest[:, None], (slot_count, cols))
    return pl.pallas_call(
        spread_kernel,
        in_specs=[smem, vmem, vmem],
        out_specs=vmem,
        out_shape=jax.ShapeDtypeStruct((2, piece, 2, slot_count, cols), jnp.bfloat16),
        compiler_params=roomy,
    )(place, lowest, owned)


def solution(mesh):
    placed = (P("wave", "lat", "lev"), P("wave", "lat", None, "lev"), P("wave"))
    return jax.shard_map(
        shards,
        mesh=mesh,
        in_specs=placed,
        out_specs=P(None, "lat", None, "wave", "lev"),
        check_vma=False,
    )
```

time: 193 us -> 183 us (0.948)
  local copies, waits for them, and re-layouts: 26 us -> 14.3 us
  Pallas kernels: 15.7 us -> 25.8 us
  waiting for transfers between devices: 98.9 us -> 93.4 us
  starting transfers between devices: 50.4 us -> 47.8 us
    pallas_call x3 -> x4, Pallas kernels: 9.98 us -> 20.1 us  [the longest x1 7.42 us: shards(): pl.pallas_call(transform_kernel, in_specs=[smem, any_space, any_space], o...]
    all_to_all x1, waiting for transfers between devices: 35.7 us -> 28.1 us  [shards(): fields = lax.all_to_all(handled, ('lat', 'lev'), 0, 0, tiled=True)]
    all_to_all x1, waiting for transfers between devices: 0.21 us -> 7.15 us  [shards(): lax.all_to_all(listing.reshape(blocks, -1), 'wave', 0, 0, tiled=True)]
    ppermute x12 -> x11, waiting for transfers between devices: 41.8 us -> 36.9 us  [the longest x10 36.9 us: hopped(): lax.ppermute(array, 'lat', [(i, band_to(i, hop)) for i in range(bands)])]
    pallas_call x7 -> x0, local copies, waits for them, and re-layouts: 4.41 us -> none  [shards(): pl.pallas_call(rest_kernel, in_specs=[smem] + [vmem] * 3, out_specs=[vmem...]
    slice x2 -> x0, local copies, waits for them, and re-layouts: 3.49 us -> none  [the longest x1 2.36 us: shards(): wide = legendre[24:28, :, :, reach // 2:]]
    ppermute x12 -> x11, starting transfers between devices: 20.9 us -> 17.8 us  [the longest x10 16.5 us: hopped(): lax.ppermute(array, 'lat', [(i, band_to(i, hop)) for i in range(bands)])]
    optimization_barrier x4 -> x0, local copies, waits for them, and re-layouts: 2.19 us -> none  [the longest x3 1.2 us: shards(): lax.optimization_barrier((outgoing, wide, slim, *first))]
  transfers between devices with their start and end apart: 16 -> 15, of which waited for: 7 -> 5; matrix products, arithmetic and copies ran while one was open for 6% -> 2% of each run, Pallas kernels for 2% -> 6%
where the time goes in v2:
time: 183 us
  waiting for transfers between devices  93.4 us (51%)
  starting transfers between devices  47.8 us (26%)
  Pallas kernels  25.8 us (14%)
  local copies, waits for them, and re-layouts  14.3 us (8%)
    ppermute x10, waiting for transfers between devices, hopped(): lax.ppermute(array, 'lat', [(i, band_to(i, hop)) for i in range(bands)])  36.9 us
    all_to_all x1, waiting for transfers between devices, shards(): fields = lax.all_to_all(handled, ('lat', 'lev'), 0, 0, tiled=True)  28.1 us
    all_to_all x1, waiting for transfers between devices, shards(): owned = lax.all_to_all(coefficients, ('lat', 'lev'), 0, 0, tiled=True)  21.3 us
    ppermute x10, starting transfers between devices, hopped(): lax.ppermute(array, 'lat', [(i, band_to(i, hop)) for i in range(bands)])  16.5 us
    unnamed x24, local copies, waits for them, and re-layouts  9.79 us
    all_to_all x1, starting transfers between devices, shards(): lax.all_to_all(listing.reshape(blocks, -1), 'wave', 0, 0, tiled=True)  9.22 us
    all_to_all x1, starting transfers between devices, shards(): arrived = lax.all_to_all(outgoing, 'wave', 0, 0, tiled=True)  8.93 us
    pallas_call x1, Pallas kernels, shards(): pl.pallas_call(transform_kernel, in_specs=[smem, any_space, any_space], o...  7.42 us
  transfers between devices with their start and end apart: 15, of which 5 were waited for; matrix products, arithmetic and copies ran while one was open for 2% of the time, Pallas kernels for 6%

profile of v2, /device:TPU:1, one launch (start us, length us, event | category | flops | bytes accessed | tf_op | source)
XLA Modules:
  0.0 182.6 jit_solution(421159221530889966)
XLA Ops:
  0.0 0.0 copy-start
  0.0 0.6 pad_add_fusion.place
  0.6 0.0 copy-start.11
  0.6 0.0 copy-start.3
  0.6 3.9 %shard_map.46 = (bf16[2,128,2,512]{3,2,1,0:T(2,128)(2,1)}, bf16[2,128,2,512]{3,2,1,0:T(2,128)(2,1)}, bf16[2,128,2,512]{3,2,1,0:T(2,128)(2,1)}, bf16[6,128,2,256]{3,2,1,0:T(2,128)(2,1)}) custom-call(s32[2]{0:T(128)} %pad_add_fusion.place, bf16[32,128,2,512]{3,2,1,0:T(2,128)(2,1)} %table.3), custom_call_target="tpu_custom_call" | custom-call | tf_op jit(solution)/shard_map/pallas_call | solution.py:214
  4.5 1.3 collective-permute-start
  5.8 3.7 %collective-permute-start.1 = (bf16[2,128,2,512]{3,2,1,0:T(2,128)(2,1)}, bf16[2,128,2,512]{3,2,1,0:T(2,128)(2,1)S(1)}, u32[]{:S(2)}, u32[]{:S(2)}) collective-permute-start(bf16[2,128,2,512]{3,2,1,0:T(2,128)(2,1)} %get-tuple-element.59), channel_id=1, source_target_pairs={{0,64},{32,224},{64,0},{96,160},{128,192},{160,96},{192,128},{224,... | collective-permute-start | bytes 1572872 | tf_op jit(solution)/shard_map/ppermute | solution.py:207
  9.4 0.0 collective-permute-start.2
  9.4 1.3 collective-permute-start.3
  10.7 0.0 copy-done.11
  10.7 0.7 all_to_all.17
  11.4 9.2 %all-to-all-start = ((s32[16,1,2]{2,1,0:T(1,128)}), s32[16,1,2]{2,1,0:T(1,128)S(1)}, u32[]{:S(2)}, u32[]{:S(2)}) async-start(s32[16,1,2]{2,1,0:T(1,128)} %bitcast.3), calls=%async_computation | async-start | bytes 16384 | tf_op jit(solution)/shard_map/all_to_all | solution.py:226
  20.6 7.1 %all-to-all-done = s32[16,1,2]{2,1,0:T(1,128)S(1)} async-done(((s32[16,1,2]{2,1,0:T(1,128)}), s32[16,1,2]{2,1,0:T(1,128)S(1)}, u32[]{:S(2)}, u32[]{:S(2)}) %all-to-all-start) | async-done | bytes 160 | tf_op jit(solution)/shard_map/all_to_all | solution.py:226
  27.8 0.1 copy.10
  27.8 0.0 collective-permute-done.cross
  27.9 0.0 copy-done.3
  27.9 4.7 %shard_map.47 = (bf16[128,2,512]{2,1,0:T(2,128)(2,1)S(1)}, bf16[128,2,512]{2,1,0:T(2,128)(2,1)S(1)}, bf16[128,2,512]{2,1,0:T(2,128)(2,1)S(1)}, bf16[3,128,2,512]...) custom-call(s32[2]{0:T(128)S(1)} %copy-done.3, ...), custom_call_target="tpu_custom_call" | custom-call | flops 1000000000 | bytes 1048576 | tf_op jit(solution)/shard_map/pallas_call | solution.py:228
  32.5 0.0 copy-start.6
  32.6 0.7 copy-done.6
  33.3 0.7 copy-done.9
  34.0 0.7 copy-done.10
  34.7 0.1 copy.11
  34.8 0.1 reshape.22
  34.9 0.0 copy-done
  34.9 2.1 %gather_fusion.1 = bf16[32,256,128]{2,1,0:T(8,128)(2,1)} fusion(bf16[32,256,128]{2,1,0:T(8,128)(2,1)S(1)} %copy-done, s32[1024]{0:T(1024)S(1)} %pad_clamp_fusion), kind=kCustom, calls=%fused_computation.1 | custom fusion | bytes 4194432 | tf_op jit(solution)/shard_map/jit(_take)/gather | solution.py:239
  37.0 0.0 collective-permute-done.1.refs_0_
  37.0 0.0 collective-permute-done.2.refs_1_
  37.0 0.0 collective-permute-done.3.refs_2_
  37.1 8.9 %all-to-all-start.1 = ((bf16[32,256,128]{2,1,0:T(8,128)(2,1)}), bf16[32,256,128]{2,1,0:T(8,128)(2,1)}, u32[]{:S(2)}, u32[]{:S(2)}) async-start(bf16[32,256,128]{2,1,0:T(8,128)(2,1)} %gather_fusion.1), calls=%async_computation.1 | async-start | bytes 4194304 | tf_op jit(solution)/shard_map/all_to_all | solution.py:241
  46.0 3.0 %collective-permute-start.10 = (bf16[128,2,512]{2,1,0:T(2,128)(2,1)}, bf16[128,2,512]{2,1,0:T(2,128)(2,1)S(1)}, u32[]{:S(2)}, u32[]{:S(2)}) collective-permute-start(bf16[128,2,512]{2,1,0:T(2,128)(2,1)} %copy-done.10), channel_id=1, source_target_pairs={{0,128},{32,160},{64,192},{96,224},{128,0},{160,32},{192,64},{224,... | collective-permute-start | bytes 786440 | tf_op jit(solution)/shard_map/ppermute | solution.py:207
  49.0 2.8 %collective-permute-start.4 = (bf16[3,128,2,512]{3,2,1,0:T(2,128)(2,1)}, bf16[3,128,2,512]{3,2,1,0:T(2,128)(2,1)}, u32[]{:S(2)}, u32[]{:S(2)}) collective-permute-start(bf16[3,128,2,512]{3,2,1,0:T(2,128)(2,1)} %get-tuple-element.67), channel_id=1, source_target_pairs={{0,96},{32,192},{64,32},{96,128},{128,224},{160,64},{192,160},{224... | collective-permute-start | bytes 2359304 | tf_op jit(solution)/shard_map/ppermute | solution.py:207
  51.8 0.0 collective-permute-start.5
  51.8 1.0 collective-permute-start.6
  52.8 1.3 collective-permute-start.7
  54.1 0.0 collective-permute-done.10.refs_5_
  54.1 0.7 copy-done.4
  54.8 2.4 %collective-permute-start.8 = (bf16[128,2,512]{2,1,0:T(2,128)(2,1)}, bf16[128,2,512]{2,1,0:T(2,128)(2,1)S(1)}, u32[]{:S(2)}, u32[]{:S(2)}) collective-permute-start(bf16[128,2,512]{2,1,0:T(2,128)(2,1)} %copy-done.9), channel_id=1, source_target_pairs={{0,64},{32,224},{64,0},{96,160},{128,192},{160,96},{192,128},{224,... | collective-permute-start | bytes 786440 | tf_op jit(solution)/shard_map/ppermute | solution.py:207
  57.2 35.7 %collective-permute-done.8.refs_3_ = bf16[128,2,512]{2,1,0:T(2,128)(2,1)S(1)} collective-permute-done((bf16[128,2,512]{2,1,0:T(2,128)(2,1)}, bf16[128,2,512]{2,1,0:T(2,128)(2,1)S(1)}, u32[]{:S(2)}, u32[]{:S(2)}) %collective-permute-start.8) | collective-permute-done | bytes 262176 | tf_op jit(solution)/shard_map/ppermute | solution.py:207
  93.0 0.7 copy-done.7
  93.7 1.1 collective-permute-start.9
  94.7 0.0 all-to-all-done.1.arrived
  94.8 1.9 %shard_map.48 = bf16[16,3,256,128]{3,2,1,0:T(8,128)(2,1)S(1)} custom-call(bf16[32,256,128]{2,1,0:T(8,128)(2,1)} %all-to-all-done.1.arrived), custom_call_target="tpu_custom_call" | custom-call | tf_op jit(solution)/shard_map/pallas_call | solution.py:249
  96.7 0.0 copy-start.1
  96.7 1.7 copy-done.1
  98.4 1.1 collective-permute-done.9.refs_4_
  99.5 0.0 collective-permute-done.4.refs_7_
  99.5 0.0 collective-permute-done.5.refs_8_
  99.5 0.0 collective-permute-done.6.refs_9_
  99.5 0.0 collective-permute-done.7.refs_10_
  99.5 6.8 %all-to-all-start.2 = ((bf16[16,3,256,128]{3,2,1,0:T(8,128)(2,1)}), bf16[16,3,256,128]{3,2,1,0:T(8,128)(2,1)}, u32[]{:S(2)}, u32[]{:S(2)}) async-start(bf16[16,3,256,128]{3,2,1,0:T(8,128)(2,1)} %copy-done.1), calls=%async_computation.2 | async-start | bytes 6291456 | tf_op jit(solution)/shard_map/all_to_all | solution.py:257
  106.3 0.7 dynamic-slice_bitcast_fusion
  107.0 0.6 gather_fusion
  107.7 0.6 pad_add_fusion.1.place
  108.2 0.9 copy-done.5
  109.2 0.9 copy-done.8
  110.1 4.1 %shard_map.49.refs_0_ = bf16[3,2,1024,512]{3,2,1,0:T(8,128)(2,1)S(1)} custom-call(bf16[2,128,2,512]{3,2,1,0:T(2,128)(2,1)S(1)} %collective-permute-done.1.refs_0_, bf16[2,128,2,512]{3,2,1,0:T(2,128)(2,1)} %collective-permute-done.2.refs_1_, bf16[2,128,2,512]{3,2,1,0:T(2,128)(2,1)} %collective-permute-done.3.refs_2_, bf16[128,2,512]{2,1,0:T(2,128)(2,1)S(1)} %copy-done.8, ...), custom_call_target="tpu_custom_call" | custom-call | flops 20000000000 | bytes 25165824 | tf_op jit(solution)/shard_map/pallas_call | solution.py:259
  114.2 0.0 copy-start.2
  114.2 2.6 %copy-done.2 = bf16[3,2,1024,512]{3,2,1,0:T(8,128)(2,1)} copy-done((bf16[3,2,1024,512]{3,2,1,0:T(8,128)(2,1)}, bf16[3,2,1024,512]{3,2,1,0:T(8,128)(2,1)S(1)}, u32[]{:S(2)}) %copy-start.2) | copy-done | bytes 6291480
  116.8 28.1 %all-to-all-done.2.refs_1_ = bf16[16,3,256,128]{3,2,1,0:T(8,128)(2,1)} async-done(((bf16[16,3,256,128]{3,2,1,0:T(8,128)(2,1)}), bf16[16,3,256,128]{3,2,1,0:T(8,128)(2,1)}, u32[]{:S(2)}, u32[]{:S(2)}) %all-to-all-start.2) | async-done | bytes 3145760 | tf_op jit(solution)/shard_map/all_to_all | solution.py:257
  144.9 7.4 %shard_map.50 = bf16[16,3,2,64,128]{4,3,2,1,0:T(8,128)(2,1)} custom-call(s32[5]{0:T(128)} %pad_add_fusion.1.place, bf16[3,2,1024,512]{3,2,1,0:T(8,128)(2,1)} %copy-done.2, bf16[16,3,256,128]{3,2,1,0:T(8,128)(2,1)} %all-to-all-done.2.refs_1_), custom_call_target="tpu_custom_call" | custom-call | tf_op jit(solution)/shard_map/pallas_call | solution.py:274
  152.4 5.1 %all-to-all-start.3 = ((bf16[16,3,2,64,128]{4,3,2,1,0:T(8,128)(2,1)}), bf16[16,3,2,64,128]{4,3,2,1,0:T(8,128)(2,1)}, u32[]{:S(2)}, u32[]{:S(2)}) async-start(bf16[16,3,2,64,128]{4,3,2,1,0:T(8,128)(2,1)} %shard_map.50), calls=%async_computation.3 | async-start | bytes 3145728 | tf_op jit(solution)/shard_map/all_to_all | solution.py:288
  157.5 21.3 %all-to-all-done.3.owned = bf16[16,3,2,64,128]{4,3,2,1,0:T(8,128)(2,1)} async-done(((bf16[16,3,2,64,128]{4,3,2,1,0:T(8,128)(2,1)}), bf16[16,3,2,64,128]{4,3,2,1,0:T(8,128)(2,1)}, u32[]{:S(2)}, u32[]{:S(2)}) %all-to-all-start.3) | async-done | bytes 1572896 | tf_op jit(solution)/shard_map/all_to_all | solution.py:288
  178.7 0.1 broadcast_in_dim.14.lowest
  178.8 3.8 %shard_map.51 = bf16[2,64,2,32,128]{4,3,2,1,0:T(8,128)(2,1)} custom-call(s32[2]{0:T(128)S(1)} %copy-done.3, s32[32,128]{1,0:T(8,128)S(1)} %broadcast_in_dim.14.lowest, bf16[16,3,2,64,128]{4,3,2,1,0:T(8,128)(2,1)} %all-to-all-done.3.owned), custom_call_target="tpu_custom_call" | custom-call | tf_op jit(solution)/shard_map/pallas_call | solution.py:292
  (11 shorter events, 0.0 us)
Async XLA Ops:
  0.0 34.9 %copy-start = (bf16[32,256,128]{2,1,0:T(8,128)(2,1)S(1)}, bf16[32,256,128]{2,1,0:T(8,128)(2,1)}, u32[]{:S(2)}) copy-start(bf16[32,256,128]{2,1,0:T(8,128)(2,1)} %param.4) | copy-start | bytes 6291460
  0.6 10.1 %copy-start.11 = (s32[32]{0:T(128)S(1)}, s32[32]{0:T(128)}, u32[]{:S(2)}) copy-start(s32[32]{0:T(128)} %param.6) | copy-start | bytes 388
  0.6 27.3 %copy-start.3 = (s32[2]{0:T(128)S(1)}, s32[2]{0:T(128)}, u32[]{:S(2)}) copy-start(s32[2]{0:T(128)} %pad_add_fusion.place) | copy-start | bytes 28
  4.5 23.4 %collective-permute-start = (bf16[6,128,2,256]{3,2,1,0:T(2,128)(2,1)}, bf16[6,128,2,256]{3,2,1,0:T(2,128)(2,1)}, u32[]{:S(2)}, u32[]{:S(2)}) collective-permute-start(bf16[6,128,2,256]{3,2,1,0:T(2,128)(2,1)} %get-tuple-element.49), channel_id=1, source_target_pairs={{1,0},{3,2},{5,4},{7,6},{9,8},{11,10},{13,12},{15,14},{17,16},{19,... | collective-permute-start | bytes 2359304 | tf_op jit(solution)/shard_map/ppermute | solution.py:223
  5.8 31.3 %collective-permute-start.1 = (bf16[2,128,2,512]{3,2,1,0:T(2,128)(2,1)}, bf16[2,128,2,512]{3,2,1,0:T(2,128)(2,1)S(1)}, u32[]{:S(2)}, u32[]{:S(2)}) collective-permute-start(bf16[2,128,2,512]{3,2,1,0:T(2,128)(2,1)} %get-tuple-element.59), channel_id=1, source_target_pairs={{0,64},{32,224},{64,0},{96,160},{128,192},{160,96},{192,128},{224,... | collective-permute-start | bytes 1572872 | tf_op jit(solution)/shard_map/ppermute | solution.py:207
  9.4 27.6 %collective-permute-start.2 = (bf16[2,128,2,512]{3,2,1,0:T(2,128)(2,1)}, bf16[2,128,2,512]{3,2,1,0:T(2,128)(2,1)}, u32[]{:S(2)}, u32[]{:S(2)}) collective-permute-start(bf16[2,128,2,512]{3,2,1,0:T(2,128)(2,1)} %get-tuple-element.60), channel_id=1, source_target_pairs={{0,192},{32,96},{64,128},{96,32},{128,64},{160,224},{192,0},{224,1... | collective-permute-start | bytes 1572872 | tf_op jit(solution)/shard_map/ppermute | solution.py:207
  9.4 27.6 %collective-permute-start.3 = (bf16[2,128,2,512]{3,2,1,0:T(2,128)(2,1)}, bf16[2,128,2,512]{3,2,1,0:T(2,128)(2,1)}, u32[]{:S(2)}, u32[]{:S(2)}) collective-permute-start(bf16[2,128,2,512]{3,2,1,0:T(2,128)(2,1)} %get-tuple-element.61), channel_id=1, source_target_pairs={{0,128},{32,160},{64,192},{96,224},{128,0},{160,32},{192,64},{224,... | collective-permute-start | bytes 1572872 | tf_op jit(solution)/shard_map/ppermute | solution.py:207
  11.4 16.4 %all-to-all-start = ((s32[16,1,2]{2,1,0:T(1,128)}), s32[16,1,2]{2,1,0:T(1,128)S(1)}, u32[]{:S(2)}, u32[]{:S(2)}) async-start(s32[16,1,2]{2,1,0:T(1,128)} %bitcast.3), calls=%async_computation | async-start | bytes 16384 | tf_op jit(solution)/shard_map/all_to_all | solution.py:226
  32.5 0.7 copy-start.6
  33.3 0.7 copy-start.9
  34.0 0.7 copy-start.10
  37.1 57.7 %all-to-all-start.1 = ((bf16[32,256,128]{2,1,0:T(8,128)(2,1)}), bf16[32,256,128]{2,1,0:T(8,128)(2,1)}, u32[]{:S(2)}, u32[]{:S(2)}) async-start(bf16[32,256,128]{2,1,0:T(8,128)(2,1)} %gather_fusion.1), calls=%async_computation.1 | async-start | bytes 4194304 | tf_op jit(solution)/shard_map/all_to_all | solution.py:241
  46.0 8.1 %collective-permute-start.10 = (bf16[128,2,512]{2,1,0:T(2,128)(2,1)}, bf16[128,2,512]{2,1,0:T(2,128)(2,1)S(1)}, u32[]{:S(2)}, u32[]{:S(2)}) collective-permute-start(bf16[128,2,512]{2,1,0:T(2,128)(2,1)} %copy-done.10), channel_id=1, source_target_pairs={{0,128},{32,160},{64,192},{96,224},{128,0},{160,32},{192,64},{224,... | collective-permute-start | bytes 786440 | tf_op jit(solution)/shard_map/ppermute | solution.py:207
  49.0 50.5 %collective-permute-start.4 = (bf16[3,128,2,512]{3,2,1,0:T(2,128)(2,1)}, bf16[3,128,2,512]{3,2,1,0:T(2,128)(2,1)}, u32[]{:S(2)}, u32[]{:S(2)}) collective-permute-start(bf16[3,128,2,512]{3,2,1,0:T(2,128)(2,1)} %get-tuple-element.67), channel_id=1, source_target_pairs={{0,96},{32,192},{64,32},{96,128},{128,224},{160,64},{192,160},{224... | collective-permute-start | bytes 2359304 | tf_op jit(solution)/shard_map/ppermute | solution.py:207
  51.8 47.7 %collective-permute-start.5 = (bf16[3,128,2,512]{3,2,1,0:T(2,128)(2,1)}, bf16[3,128,2,512]{3,2,1,0:T(2,128)(2,1)}, u32[]{:S(2)}, u32[]{:S(2)}) collective-permute-start(bf16[3,128,2,512]{3,2,1,0:T(2,128)(2,1)} %get-tuple-element.68), channel_id=1, source_target_pairs={{0,224},{32,64},{64,160},{96,0},{128,96},{160,192},{192,32},{224,1... | collective-permute-start | bytes 2359304 | tf_op jit(solution)/shard_map/ppermute | solution.py:207
  51.8 47.7 %collective-permute-start.6 = (bf16[3,128,2,512]{3,2,1,0:T(2,128)(2,1)}, bf16[3,128,2,512]{3,2,1,0:T(2,128)(2,1)}, u32[]{:S(2)}, u32[]{:S(2)}) collective-permute-start(bf16[3,128,2,512]{3,2,1,0:T(2,128)(2,1)} %get-tuple-element.69), channel_id=1, source_target_pairs={{0,160},{32,128},{64,224},{96,192},{128,32},{160,0},{192,96},{224,... | collective-permute-start | bytes 2359304 | tf_op jit(solution)/shard_map/ppermute | solution.py:207
  52.8 46.7 %collective-permute-start.7 = (bf16[3,128,2,512]{3,2,1,0:T(2,128)(2,1)}, bf16[3,128,2,512]{3,2,1,0:T(2,128)(2,1)}, u32[]{:S(2)}, u32[]{:S(2)}) collective-permute-start(bf16[3,128,2,512]{3,2,1,0:T(2,128)(2,1)} %get-tuple-element.70), channel_id=1, source_target_pairs={{0,32},{32,0},{64,96},{96,64},{128,160},{160,128},{192,224},{224,1... | collective-permute-start | bytes 2359304 | tf_op jit(solution)/shard_map/ppermute | solution.py:207
  54.1 0.7 copy-start.4
  54.8 38.2 %collective-permute-start.8 = (bf16[128,2,512]{2,1,0:T(2,128)(2,1)}, bf16[128,2,512]{2,1,0:T(2,128)(2,1)S(1)}, u32[]{:S(2)}, u32[]{:S(2)}) collective-permute-start(bf16[128,2,512]{2,1,0:T(2,128)(2,1)} %copy-done.9), channel_id=1, source_target_pairs={{0,64},{32,224},{64,0},{96,160},{128,192},{160,96},{192,128},{224,... | collective-permute-start | bytes 786440 | tf_op jit(solution)/shard_map/ppermute | solution.py:207
  93.0 0.7 copy-start.7
  93.7 5.8 %collective-permute-start.9 = (bf16[128,2,512]{2,1,0:T(2,128)(2,1)}, bf16[128,2,512]{2,1,0:T(2,128)(2,1)}, u32[]{:S(2)}, u32[]{:S(2)}) collective-permute-start(bf16[128,2,512]{2,1,0:T(2,128)(2,1)} %copy-done.6), channel_id=1, source_target_pairs={{0,192},{32,96},{64,128},{96,32},{128,64},{160,224},{192,0},{224,1... | collective-permute-start | bytes 786440 | tf_op jit(solution)/shard_map/ppermute | solution.py:207
  96.7 1.7 copy-start.1
  99.5 45.4 %all-to-all-start.2 = ((bf16[16,3,256,128]{3,2,1,0:T(8,128)(2,1)}), bf16[16,3,256,128]{3,2,1,0:T(8,128)(2,1)}, u32[]{:S(2)}, u32[]{:S(2)}) async-start(bf16[16,3,256,128]{3,2,1,0:T(8,128)(2,1)} %copy-done.1), calls=%async_computation.2 | async-start | bytes 6291456 | tf_op jit(solution)/shard_map/all_to_all | solution.py:257
  108.2 0.9 copy-start.5
  109.2 0.9 copy-start.8
  114.2 2.6 %copy-start.2 = (bf16[3,2,1024,512]{3,2,1,0:T(8,128)(2,1)}, bf16[3,2,1024,512]{3,2,1,0:T(8,128)(2,1)S(1)}, u32[]{:S(2)}) copy-start(bf16[3,2,1024,512]{3,2,1,0:T(8,128)(2,1)S(1)} %shard_map.49.refs_0_) | copy-start | bytes 18874372
  152.4 26.4 %all-to-all-start.3 = ((bf16[16,3,2,64,128]{4,3,2,1,0:T(8,128)(2,1)}), bf16[16,3,2,64,128]{4,3,2,1,0:T(8,128)(2,1)}, u32[]{:S(2)}, u32[]{:S(2)}) async-start(bf16[16,3,2,64,128]{4,3,2,1,0:T(8,128)(2,1)} %shard_map.50), calls=%async_computation.3 | async-start | bytes 3145728 | tf_op jit(solution)/shard_map/all_to_all | solution.py:288

commit v3 on v2

--- a/solution.py
+++ b/solution.py
@@ -181,13 +181,12 @@
     for k in range(2):
         count = len(whole[k])
         q = lax.broadcasted_iota(jnp.int32, (piece, count, cols), 0) + (8 * k + place[0]) * piece
-        for p in range(2):
-            held = jnp.stack([owned[n, e, p].astype(jnp.float32) for n, e in whole[k]])
-            held = jnp.transpose(held, (1, 0, 2))
-            held = jnp.where(2 * q + p >= lowest[0:count][None], held, 0.0)
-            out[k, :, p, 0:count] = held.astype(jnp.bfloat16)
-            if count < slots:
-                out[k, :, p, count:] = jnp.zeros((piece, slots - count, cols), jnp.bfloat16)
+        held = jnp.stack([owned[n, e, 0].astype(jnp.float32) for n, e in whole[k]])
+        held = jnp.transpose(held, (1, 0, 2))
+        held = jnp.where(2 * q + pl.program_id(0) >= lowest[0:count][None], held, 0.0)
+        out[k, :, 0, 0:count] = held.astype(jnp.bfloat16)
+        if count < slots:
+            out[k, :, 0, count:] = jnp.zeros((piece, slots - count, cols), jnp.bfloat16)
 
 
 def shards(fourier, legendre, wave_list):
@@ -231,7 +230,7 @@
         out_specs=[vmem] * 8,
         out_shape=[shape_of(rows, 2, reach)] * 3 + [shape_of(3, rows, 2, reach)] * 5,
         scratch_shapes=[pltpu.SemaphoreType.DMA((8, 3))],
-        compiler_params=pltpu.CompilerParams(vmem_limit_bytes=52 * 1024 * 1024),
+        compiler_params=pltpu.CompilerParams(vmem_limit_bytes=48 * 1024 * 1024),
         cost_estimate=pl.CostEstimate(flops=10**9, bytes_accessed=2**20, transcendentals=0),
     )(place, legendre, cross)
     wanted, rest = lax.optimization_barrier((wanted, rest))
@@ -291,8 +290,13 @@
     lowest = jnp.broadcast_to(lowest[:, None], (slot_count, cols))
     return pl.pallas_call(
         spread_kernel,
-        in_specs=[smem, vmem, vmem],
-        out_specs=vmem,
+        grid=(2,),
+        in_specs=[
+            smem,
+            pl.BlockSpec((slot_count, cols), lambda p: (0, 0)),
+            pl.BlockSpec((2 * bands, 3, 1, piece, cols), lambda p: (0, 0, p, 0, 0)),
+        ],
+        out_specs=pl.BlockSpec((2, piece, 1, slot_count, cols), lambda p: (0, 0, p, 0, 0)),
         out_shape=jax.ShapeDtypeStruct((2, piece, 2, slot_count, cols), jnp.bfloat16),
         compiler_params=roomy,
     )(place, lowest, owned)

time: 183 us -> 183 us (level)
    unnamed x24 -> x30, local copies, waits for them, and re-layouts: 9.79 us -> 9.93 us
where the time goes in v3:
time: 183 us; the launch traced here: 182 us
  waiting for transfers between devices  93.4 us (51%)
  starting transfers between devices  48.4 us (26%)
  Pallas kernels  24.7 us (13%)
  local copies, waits for them, and re-layouts  14.4 us (8%)
    ppermute x10, waiting for transfers between devices, hopped(): lax.ppermute(array, 'lat', [(i, band_to(i, hop)) for i in range(bands)])  36.8 us
    all_to_all x1, waiting for transfers between devices, shards(): fields = lax.all_to_all(handled, ('lat', 'lev'), 0, 0, tiled=True)  28 us
    all_to_all x1, waiting for transfers between devices, shards(): owned = lax.all_to_all(coefficients, ('lat', 'lev'), 0, 0, tiled=True)  21.3 us
    ppermute x10, starting transfers between devices, hopped(): lax.ppermute(array, 'lat', [(i, band_to(i, hop)) for i in range(bands)])  16.4 us
    unnamed x30, local copies, waits for them, and re-layouts  9.93 us
    all_to_all x1, starting transfers between devices, shards(): lax.all_to_all(listing.reshape(blocks, -1), 'wave', 0, 0, tiled=True)  9.22 us
    all_to_all x1, starting transfers between devices, shards(): arrived = lax.all_to_all(outgoing, 'wave', 0, 0, tiled=True)  8.9 us
    all_to_all x1, starting transfers between devices, shards(): fields = lax.all_to_all(handled, ('lat', 'lev'), 0, 0, tiled=True)  7.54 us
  transfers between devices with their start and end apart: 15, of which 5 were waited for; matrix products, arithmetic and copies ran while one was open for 2% of the time, Pallas kernels for 6%

profile of v3, /device:TPU:1, one launch (start us, length us, event | category | flops | bytes accessed | tf_op | source)
XLA Modules:
  0.0 182.4 jit_solution(13333275117433113122)
XLA Ops:
  0.0 0.0 copy-start
  0.0 0.6 pad_add_fusion.place
  0.6 3.9 %shard_map.46 = (bf16[2,128,2,512]{3,2,1,0:T(2,128)(2,1)}, bf16[2,128,2,512]{3,2,1,0:T(2,128)(2,1)}, bf16[2,128,2,512]{3,2,1,0:T(2,128)(2,1)}, bf16[6,128,2,256]{3,2,1,0:T(2,128)(2,1)}) custom-call(s32[2]{0:T(128)} %pad_add_fusion.place, bf16[32,128,2,512]{3,2,1,0:T(2,128)(2,1)} %table.3), custom_call_target="tpu_custom_call" | custom-call | tf_op jit(solution)/shard_map/pallas_call | solution.py:213
  4.5 1.3 collective-permute-start
  5.8 3.7 %collective-permute-start.1 = (bf16[2,128,2,512]{3,2,1,0:T(2,128)(2,1)}, bf16[2,128,2,512]{3,2,1,0:T(2,128)(2,1)S(1)}, u32[]{:S(2)}, u32[]{:S(2)}) collective-permute-start(bf16[2,128,2,512]{3,2,1,0:T(2,128)(2,1)} %get-tuple-element.59), channel_id=1, source_target_pairs={{0,64},{32,224},{64,0},{96,160},{128,192},{160,96},{192,128},{224,... | collective-permute-start | bytes 1572872 | tf_op jit(solution)/shard_map/ppermute | solution.py:206
  9.4 0.0 collective-permute-start.2
  9.4 1.3 collective-permute-start.3
  10.7 0.0 copy-done.14
  10.7 0.7 all_to_all.17
  11.4 9.2 %all-to-all-start = ((s32[16,1,2]{2,1,0:T(1,128)}), s32[16,1,2]{2,1,0:T(1,128)S(1)}, u32[]{:S(2)}, u32[]{:S(2)}) async-start(s32[16,1,2]{2,1,0:T(1,128)} %bitcast.3), calls=%async_computation | async-start | bytes 16384 | tf_op jit(solution)/shard_map/all_to_all | solution.py:225
  20.6 7.3 %all-to-all-done = s32[16,1,2]{2,1,0:T(1,128)S(1)} async-done(((s32[16,1,2]{2,1,0:T(1,128)}), s32[16,1,2]{2,1,0:T(1,128)S(1)}, u32[]{:S(2)}, u32[]{:S(2)}) %all-to-all-start) | async-done | bytes 160 | tf_op jit(solution)/shard_map/all_to_all | solution.py:225
  27.9 0.1 copy.10
  28.0 0.0 collective-permute-done.cross
  28.0 0.0 copy-done.3
  28.0 4.2 %shard_map.47 = (bf16[128,2,512]{2,1,0:T(2,128)(2,1)S(1)}, bf16[128,2,512]{2,1,0:T(2,128)(2,1)}, bf16[128,2,512]{2,1,0:T(2,128)(2,1)S(1)}, bf16[3,128,2,512]{3,2...) custom-call(s32[2]{0:T(128)S(1)} %copy-done.3, ...), custom_call_target="tpu_custom_call" | custom-call | flops 1000000000 | bytes 1048576 | tf_op jit(solution)/shard_map/pallas_call | solution.py:227
  32.2 0.0 copy-start.4
  32.2 0.9 copy-done.4
  33.1 0.7 copy-done.10
  33.8 0.7 copy-done.12
  34.5 0.1 copy.11
  34.6 0.1 reshape.22
  34.7 0.0 copy-done
  34.7 2.1 %gather_fusion.1 = bf16[32,256,128]{2,1,0:T(8,128)(2,1)} fusion(bf16[32,256,128]{2,1,0:T(8,128)(2,1)S(1)} %copy-done, s32[1024]{0:T(1024)S(1)} %pad_clamp_fusion), kind=kCustom, calls=%fused_computation.1 | custom fusion | bytes 4194432 | tf_op jit(solution)/shard_map/jit(_take)/gather | solution.py:238
  36.8 0.0 collective-permute-done.1.refs_0_
  36.8 0.0 collective-permute-done.2.refs_1_
  36.9 0.0 collective-permute-done.3.refs_2_
  36.9 8.9 %all-to-all-start.1 = ((bf16[32,256,128]{2,1,0:T(8,128)(2,1)}), bf16[32,256,128]{2,1,0:T(8,128)(2,1)}, u32[]{:S(2)}, u32[]{:S(2)}) async-start(bf16[32,256,128]{2,1,0:T(8,128)(2,1)} %gather_fusion.1), calls=%async_computation.1 | async-start | bytes 4194304 | tf_op jit(solution)/shard_map/all_to_all | solution.py:240
  45.8 0.0 copy-done.13
  45.8 3.0 %collective-permute-start.10 = (bf16[128,2,512]{2,1,0:T(2,128)(2,1)S(1)}, bf16[128,2,512]{2,1,0:T(2,128)(2,1)S(1)}, u32[]{:S(2)}, u32[]{:S(2)}) collective-permute-start(bf16[128,2,512]{2,1,0:T(2,128)(2,1)S(1)} %copy-done.13), channel_id=1, source_target_pairs={{0,128},{32,160},{64,192},{96,224},{128,0},{160,32},{192,64},{224,... | collective-permute-start | bytes 786440 | tf_op jit(solution)/shard_map/ppermute | solution.py:206
  48.8 2.7 %collective-permute-start.4 = (bf16[3,128,2,512]{3,2,1,0:T(2,128)(2,1)}, bf16[3,128,2,512]{3,2,1,0:T(2,128)(2,1)}, u32[]{:S(2)}, u32[]{:S(2)}) collective-permute-start(bf16[3,128,2,512]{3,2,1,0:T(2,128)(2,1)} %get-tuple-element.67), channel_id=1, source_target_pairs={{0,96},{32,192},{64,32},{96,128},{128,224},{160,64},{192,160},{224... | collective-permute-start | bytes 2359304 | tf_op jit(solution)/shard_map/ppermute | solution.py:206
  51.5 0.0 collective-permute-start.5
  51.5 1.0 collective-permute-start.6
  52.5 1.3 collective-permute-start.7
  53.8 0.0 collective-permute-done.10.refs_5_
  53.8 0.7 copy-done.6
  54.4 0.0 copy-done.11
  54.5 2.4 %collective-permute-start.8 = (bf16[128,2,512]{2,1,0:T(2,128)(2,1)S(1)}, bf16[128,2,512]{2,1,0:T(2,128)(2,1)S(1)}, u32[]{:S(2)}, u32[]{:S(2)}) collective-permute-start(bf16[128,2,512]{2,1,0:T(2,128)(2,1)S(1)} %copy-done.11), channel_id=1, source_target_pairs={{0,64},{32,224},{64,0},{96,160},{128,192},{160,96},{192,128},{224,... | collective-permute-start | bytes 786440 | tf_op jit(solution)/shard_map/ppermute | solution.py:206
  56.9 35.7 %collective-permute-done.8.refs_3_ = bf16[128,2,512]{2,1,0:T(2,128)(2,1)S(1)} collective-permute-done((bf16[128,2,512]{2,1,0:T(2,128)(2,1)S(1)}, bf16[128,2,512]{2,1,0:T(2,128)(2,1)S(1)}, u32[]{:S(2)}, u32[]{:S(2)}) %collective-permute-start.8) | collective-permute-done | bytes 262176 | tf_op jit(solution)/shard_map/ppermute | solution.py:206
  92.5 0.7 copy-done.8
  93.2 1.1 collective-permute-start.9
  94.3 0.0 all-to-all-done.1.arrived
  94.3 1.9 %shard_map.48 = bf16[16,3,256,128]{3,2,1,0:T(8,128)(2,1)S(1)} custom-call(bf16[32,256,128]{2,1,0:T(8,128)(2,1)} %all-to-all-done.1.arrived), custom_call_target="tpu_custom_call" | custom-call | tf_op jit(solution)/shard_map/pallas_call | solution.py:248
  96.3 0.0 copy-start.1
  96.3 1.7 copy-done.1
  98.0 1.1 collective-permute-done.9.refs_4_
  99.1 0.0 collective-permute-done.4.refs_7_
  99.1 0.0 collective-permute-done.5.refs_8_
  99.1 0.0 collective-permute-done.6.refs_9_
  99.1 0.0 collective-permute-done.7.refs_10_
  99.1 7.5 %all-to-all-start.2 = ((bf16[16,3,256,128]{3,2,1,0:T(8,128)(2,1)}), bf16[16,3,256,128]{3,2,1,0:T(8,128)(2,1)}, u32[]{:S(2)}, u32[]{:S(2)}) async-start(bf16[16,3,256,128]{3,2,1,0:T(8,128)(2,1)} %copy-done.1), calls=%async_computation.2 | async-start | bytes 6291456 | tf_op jit(solution)/shard_map/all_to_all | solution.py:256
  106.6 0.7 dynamic-slice_bitcast_fusion
  107.3 0.6 gather_fusion
  108.0 0.6 pad_add_fusion.1.place
  108.6 0.0 copy-done.5
  108.6 0.9 copy-done.7
  109.6 0.9 copy-done.9
  110.5 4.1 %shard_map.49.refs_0_ = bf16[3,2,1024,512]{3,2,1,0:T(8,128)(2,1)S(1)} custom-call(bf16[2,128,2,512]{3,2,1,0:T(2,128)(2,1)S(1)} %collective-permute-done.1.refs_0_, bf16[2,128,2,512]{3,2,1,0:T(2,128)(2,1)} %collective-permute-done.2.refs_1_, bf16[2,128,2,512]{3,2,1,0:T(2,128)(2,1)} %collective-permute-done.3.refs_2_, bf16[128,2,512]{2,1,0:T(2,128)(2,1)S(1)} %copy-done.9, ...), custom_call_target="tpu_custom_call" | custom-call | flops 20000000000 | bytes 25165824 | tf_op jit(solution)/shard_map/pallas_call | solution.py:258
  114.6 2.6 %copy-done.2 = bf16[3,2,1024,512]{3,2,1,0:T(8,128)(2,1)} copy-done((bf16[3,2,1024,512]{3,2,1,0:T(8,128)(2,1)}, bf16[3,2,1024,512]{3,2,1,0:T(8,128)(2,1)S(1)}, u32[]{:S(2)}) %copy-start.2) | copy-done | bytes 6291480
  117.2 28.0 %all-to-all-done.2.refs_1_ = bf16[16,3,256,128]{3,2,1,0:T(8,128)(2,1)} async-done(((bf16[16,3,256,128]{3,2,1,0:T(8,128)(2,1)}), bf16[16,3,256,128]{3,2,1,0:T(8,128)(2,1)}, u32[]{:S(2)}, u32[]{:S(2)}) %all-to-all-start.2) | async-done | bytes 3145760 | tf_op jit(solution)/shard_map/all_to_all | solution.py:256
  145.2 7.4 %shard_map.50 = bf16[16,3,2,64,128]{4,3,2,1,0:T(8,128)(2,1)} custom-call(s32[5]{0:T(128)} %pad_add_fusion.1.place, bf16[3,2,1024,512]{3,2,1,0:T(8,128)(2,1)} %copy-done.2, bf16[16,3,256,128]{3,2,1,0:T(8,128)(2,1)} %all-to-all-done.2.refs_1_), custom_call_target="tpu_custom_call" | custom-call | tf_op jit(solution)/shard_map/pallas_call | solution.py:273
  152.7 5.1 %all-to-all-start.3 = ((bf16[16,3,2,64,128]{4,3,2,1,0:T(8,128)(2,1)}), bf16[16,3,2,64,128]{4,3,2,1,0:T(8,128)(2,1)}, u32[]{:S(2)}, u32[]{:S(2)}) async-start(bf16[16,3,2,64,128]{4,3,2,1,0:T(8,128)(2,1)} %shard_map.50), calls=%async_computation.3 | async-start | bytes 3145728 | tf_op jit(solution)/shard_map/all_to_all | solution.py:287
  157.8 21.3 %all-to-all-done.3.owned = bf16[16,3,2,64,128]{4,3,2,1,0:T(8,128)(2,1)} async-done(((bf16[16,3,2,64,128]{4,3,2,1,0:T(8,128)(2,1)}), bf16[16,3,2,64,128]{4,3,2,1,0:T(8,128)(2,1)}, u32[]{:S(2)}, u32[]{:S(2)}) %all-to-all-start.3) | async-done | bytes 1572896 | tf_op jit(solution)/shard_map/all_to_all | solution.py:287
  179.1 0.1 broadcast_in_dim.14.lowest
  179.1 3.3 %shard_map.51 = bf16[2,64,2,32,128]{4,3,2,1,0:T(8,128)(2,1)} custom-call(s32[2]{0:T(128)S(1)} %copy-done.3, s32[32,128]{1,0:T(8,128)S(1)} %broadcast_in_dim.14.lowest, bf16[16,3,2,64,128]{4,3,2,1,0:T(8,128)(2,1)} %all-to-all-done.3.owned), custom_call_target="tpu_custom_call" | custom-call | tf_op jit(solution)/shard_map/pallas_call | solution.py:291
  (17 shorter events, 0.1 us)
Async XLA Ops:
  0.0 34.7 %copy-start = (bf16[32,256,128]{2,1,0:T(8,128)(2,1)S(1)}, bf16[32,256,128]{2,1,0:T(8,128)(2,1)}, u32[]{:S(2)}) copy-start(bf16[32,256,128]{2,1,0:T(8,128)(2,1)} %param.4) | copy-start | bytes 6291460
  0.6 10.1 %copy-start.14 = (s32[32]{0:T(128)S(1)}, s32[32]{0:T(128)}, u32[]{:S(2)}) copy-start(s32[32]{0:T(128)} %param.6) | copy-start | bytes 388
  0.6 27.4 %copy-start.3 = (s32[2]{0:T(128)S(1)}, s32[2]{0:T(128)}, u32[]{:S(2)}) copy-start(s32[2]{0:T(128)} %pad_add_fusion.place) | copy-start | bytes 28
  4.5 23.5 %collective-permute-start = (bf16[6,128,2,256]{3,2,1,0:T(2,128)(2,1)}, bf16[6,128,2,256]{3,2,1,0:T(2,128)(2,1)S(1)}, u32[]{:S(2)}, u32[]{:S(2)}) collective-permute-start(bf16[6,128,2,256]{3,2,1,0:T(2,128)(2,1)} %get-tuple-element.49), channel_id=1, source_target_pairs={{1,0},{3,2},{5,4},{7,6},{9,8},{11,10},{13,12},{15,14},{17,16},{19,... | collective-permute-start | bytes 2359304 | tf_op jit(solution)/shard_map/ppermute | solution.py:222
  5.8 31.1 %collective-permute-start.1 = (bf16[2,128,2,512]{3,2,1,0:T(2,128)(2,1)}, bf16[2,128,2,512]{3,2,1,0:T(2,128)(2,1)S(1)}, u32[]{:S(2)}, u32[]{:S(2)}) collective-permute-start(bf16[2,128,2,512]{3,2,1,0:T(2,128)(2,1)} %get-tuple-element.59), channel_id=1, source_target_pairs={{0,64},{32,224},{64,0},{96,160},{128,192},{160,96},{192,128},{224,... | collective-permute-start | bytes 1572872 | tf_op jit(solution)/shard_map/ppermute | solution.py:206
  9.4 27.4 %collective-permute-start.2 = (bf16[2,128,2,512]{3,2,1,0:T(2,128)(2,1)}, bf16[2,128,2,512]{3,2,1,0:T(2,128)(2,1)}, u32[]{:S(2)}, u32[]{:S(2)}) collective-permute-start(bf16[2,128,2,512]{3,2,1,0:T(2,128)(2,1)} %get-tuple-element.60), channel_id=1, source_target_pairs={{0,192},{32,96},{64,128},{96,32},{128,64},{160,224},{192,0},{224,1... | collective-permute-start | bytes 1572872 | tf_op jit(solution)/shard_map/ppermute | solution.py:206
  9.4 27.4 %collective-permute-start.3 = (bf16[2,128,2,512]{3,2,1,0:T(2,128)(2,1)}, bf16[2,128,2,512]{3,2,1,0:T(2,128)(2,1)}, u32[]{:S(2)}, u32[]{:S(2)}) collective-permute-start(bf16[2,128,2,512]{3,2,1,0:T(2,128)(2,1)} %get-tuple-element.61), channel_id=1, source_target_pairs={{0,128},{32,160},{64,192},{96,224},{128,0},{160,32},{192,64},{224,... | collective-permute-start | bytes 1572872 | tf_op jit(solution)/shard_map/ppermute | solution.py:206
  11.4 16.5 %all-to-all-start = ((s32[16,1,2]{2,1,0:T(1,128)}), s32[16,1,2]{2,1,0:T(1,128)S(1)}, u32[]{:S(2)}, u32[]{:S(2)}) async-start(s32[16,1,2]{2,1,0:T(1,128)} %bitcast.3), calls=%async_computation | async-start | bytes 16384 | tf_op jit(solution)/shard_map/all_to_all | solution.py:225
  32.2 0.9 copy-start.4
  33.1 0.7 copy-start.10
  33.8 0.7 copy-start.12
  36.8 8.9 %copy-start.13 = (bf16[128,2,512]{2,1,0:T(2,128)(2,1)S(1)}, bf16[128,2,512]{2,1,0:T(2,128)(2,1)}, u32[]{:S(2)}) copy-start(bf16[128,2,512]{2,1,0:T(2,128)(2,1)} %copy-done.12) | copy-start | bytes 786436
  36.8 17.6 %copy-start.11 = (bf16[128,2,512]{2,1,0:T(2,128)(2,1)S(1)}, bf16[128,2,512]{2,1,0:T(2,128)(2,1)}, u32[]{:S(2)}) copy-start(bf16[128,2,512]{2,1,0:T(2,128)(2,1)} %copy-done.10) | copy-start | bytes 786436
  36.9 57.5 %all-to-all-start.1 = ((bf16[32,256,128]{2,1,0:T(8,128)(2,1)}), bf16[32,256,128]{2,1,0:T(8,128)(2,1)}, u32[]{:S(2)}, u32[]{:S(2)}) async-start(bf16[32,256,128]{2,1,0:T(8,128)(2,1)} %gather_fusion.1), calls=%async_computation.1 | async-start | bytes 4194304 | tf_op jit(solution)/shard_map/all_to_all | solution.py:240
  45.8 8.0 %collective-permute-start.10 = (bf16[128,2,512]{2,1,0:T(2,128)(2,1)S(1)}, bf16[128,2,512]{2,1,0:T(2,128)(2,1)S(1)}, u32[]{:S(2)}, u32[]{:S(2)}) collective-permute-start(bf16[128,2,512]{2,1,0:T(2,128)(2,1)S(1)} %copy-done.13), channel_id=1, source_target_pairs={{0,128},{32,160},{64,192},{96,224},{128,0},{160,32},{192,64},{224,... | collective-permute-start | bytes 786440 | tf_op jit(solution)/shard_map/ppermute | solution.py:206
  48.8 50.3 %collective-permute-start.4 = (bf16[3,128,2,512]{3,2,1,0:T(2,128)(2,1)}, bf16[3,128,2,512]{3,2,1,0:T(2,128)(2,1)}, u32[]{:S(2)}, u32[]{:S(2)}) collective-permute-start(bf16[3,128,2,512]{3,2,1,0:T(2,128)(2,1)} %get-tuple-element.67), channel_id=1, source_target_pairs={{0,96},{32,192},{64,32},{96,128},{128,224},{160,64},{192,160},{224... | collective-permute-start | bytes 2359304 | tf_op jit(solution)/shard_map/ppermute | solution.py:206
  51.5 47.6 %collective-permute-start.5 = (bf16[3,128,2,512]{3,2,1,0:T(2,128)(2,1)}, bf16[3,128,2,512]{3,2,1,0:T(2,128)(2,1)}, u32[]{:S(2)}, u32[]{:S(2)}) collective-permute-start(bf16[3,128,2,512]{3,2,1,0:T(2,128)(2,1)} %get-tuple-element.68), channel_id=1, source_target_pairs={{0,224},{32,64},{64,160},{96,0},{128,96},{160,192},{192,32},{224,1... | collective-permute-start | bytes 2359304 | tf_op jit(solution)/shard_map/ppermute | solution.py:206
  51.5 47.6 %collective-permute-start.6 = (bf16[3,128,2,512]{3,2,1,0:T(2,128)(2,1)}, bf16[3,128,2,512]{3,2,1,0:T(2,128)(2,1)}, u32[]{:S(2)}, u32[]{:S(2)}) collective-permute-start(bf16[3,128,2,512]{3,2,1,0:T(2,128)(2,1)} %get-tuple-element.69), channel_id=1, source_target_pairs={{0,160},{32,128},{64,224},{96,192},{128,32},{160,0},{192,96},{224,... | collective-permute-start | bytes 2359304 | tf_op jit(solution)/shard_map/ppermute | solution.py:206
  52.5 46.6 %collective-permute-start.7 = (bf16[3,128,2,512]{3,2,1,0:T(2,128)(2,1)}, bf16[3,128,2,512]{3,2,1,0:T(2,128)(2,1)}, u32[]{:S(2)}, u32[]{:S(2)}) collective-permute-start(bf16[3,128,2,512]{3,2,1,0:T(2,128)(2,1)} %get-tuple-element.70), channel_id=1, source_target_pairs={{0,32},{32,0},{64,96},{96,64},{128,160},{160,128},{192,224},{224,1... | collective-permute-start | bytes 2359304 | tf_op jit(solution)/shard_map/ppermute | solution.py:206
  53.8 0.7 copy-start.6
  54.5 38.1 %collective-permute-start.8 = (bf16[128,2,512]{2,1,0:T(2,128)(2,1)S(1)}, bf16[128,2,512]{2,1,0:T(2,128)(2,1)S(1)}, u32[]{:S(2)}, u32[]{:S(2)}) collective-permute-start(bf16[128,2,512]{2,1,0:T(2,128)(2,1)S(1)} %copy-done.11), channel_id=1, source_target_pairs={{0,64},{32,224},{64,0},{96,160},{128,192},{160,96},{192,128},{224,... | collective-permute-start | bytes 786440 | tf_op jit(solution)/shard_map/ppermute | solution.py:206
  92.5 0.7 copy-start.8
  93.2 5.8 %collective-permute-start.9 = (bf16[128,2,512]{2,1,0:T(2,128)(2,1)}, bf16[128,2,512]{2,1,0:T(2,128)(2,1)}, u32[]{:S(2)}, u32[]{:S(2)}) collective-permute-start(bf16[128,2,512]{2,1,0:T(2,128)(2,1)} %get-tuple-element.72), channel_id=1, source_target_pairs={{0,192},{32,96},{64,128},{96,32},{128,64},{160,224},{192,0},{224,1... | collective-permute-start | bytes 786440 | tf_op jit(solution)/shard_map/ppermute | solution.py:206
  96.3 1.7 copy-start.1
  98.0 10.6 %copy-start.5 = (bf16[3,128,2,512]{3,2,1,0:T(2,128)(2,1)S(1)}, bf16[3,128,2,512]{3,2,1,0:T(2,128)(2,1)}, u32[]{:S(2)}) copy-start(bf16[3,128,2,512]{3,2,1,0:T(2,128)(2,1)} %copy-done.4) | copy-start | bytes 2359300
  99.1 46.2 %all-to-all-start.2 = ((bf16[16,3,256,128]{3,2,1,0:T(8,128)(2,1)}), bf16[16,3,256,128]{3,2,1,0:T(8,128)(2,1)}, u32[]{:S(2)}, u32[]{:S(2)}) async-start(bf16[16,3,256,128]{3,2,1,0:T(8,128)(2,1)} %copy-done.1), calls=%async_computation.2 | async-start | bytes 6291456 | tf_op jit(solution)/shard_map/all_to_all | solution.py:256
  108.6 1.0 copy-start.7
  109.6 0.9 copy-start.9
  114.6 2.6 %copy-start.2 = (bf16[3,2,1024,512]{3,2,1,0:T(8,128)(2,1)}, bf16[3,2,1024,512]{3,2,1,0:T(8,128)(2,1)S(1)}, u32[]{:S(2)}) copy-start(bf16[3,2,1024,512]{3,2,1,0:T(8,128)(2,1)S(1)} %shard_map.49.refs_0_) | copy-start | bytes 18874372
  152.7 26.4 %all-to-all-start.3 = ((bf16[16,3,2,64,128]{4,3,2,1,0:T(8,128)(2,1)}), bf16[16,3,2,64,128]{4,3,2,1,0:T(8,128)(2,1)}, u32[]{:S(2)}, u32[]{:S(2)}) async-start(bf16[16,3,2,64,128]{4,3,2,1,0:T(8,128)(2,1)} %shard_map.50), calls=%async_computation.3 | async-start | bytes 3145728 | tf_op jit(solution)/shard_map/all_to_all | solution.py:287

commit v4 on v3

--- a/solution.py
+++ b/solution.py
@@ -8,8 +8,8 @@
 from jax.sharding import PartitionSpec as P
 
 NN = 2048
-FIRST = (2, 6, 4)
-LAST = (3, 7, 5, 1)
+FIRST = (4, 2, 6)
+LAST = (5, 3, 7, 1)
 
 
 def band_to(lat, hop):
@@ -115,55 +115,49 @@
             out[f, :, hop * rows : (hop + 1) * rows, :] = jnp.swapaxes(values, 0, 1)
 
 
-def transform_kernel(place, *refs):
-    packed, arrived, out, source, table, fields, sems = refs
+def transform_kernel(place, table, fields, out, source):
     lat = place[0]
     rows, reach = table.shape[2] // 8, table.shape[3]
     width = reach // 4
     half = width // 2
-    cols = arrived.shape[3]
-    fetch = pltpu.make_async_copy(arrived, fields, sems.at[0])
-    fetch.start()
-    load = pltpu.make_async_copy(packed, table, sems.at[1])
-    load.start()
+    cols = fields.shape[3]
+    odd = place[2 + pl.program_id(0)] == 1
     at_row = lax.broadcasted_iota(jnp.int32, (rows, rows), 0)
     at_col = lax.broadcasted_iota(jnp.int32, (rows, rows), 1)
     flip = (at_row + at_col == rows - 1).astype(jnp.bfloat16)
-    fetch.wait()
-    pairs = [(f, v) for f in range(3) for v in range(2)]
     for hop in range(8):
         band = band_from(lat, hop)
-        near = [fields[2 * band + v, f, 0:rows, :] for f, v in pairs]
-        far = [fields[2 * (7 - band) + v, f, rows : 2 * rows, :] for f, v in pairs]
-        mirrored = jnp.dot(flip, jnp.concatenate(far, 1), preferred_element_type=jnp.float32)
-        for n, (f, v) in enumerate(pairs):
-            one = near[n].astype(jnp.float32)
-            other = mirrored[:, n * cols : (n + 1) * cols]
-            odd = place[2 + f] == 1
-            other = jnp.where(odd, -other, other)
-            here = (slice(hop * rows, (hop + 1) * rows), slice(v * cols, (v + 1) * cols))
-            source[f, 0, *here] = (one + other).astype(jnp.bfloat16)
-            source[f, 1, *here] = (one - other).astype(jnp.bfloat16)
-    load.wait()
-    for f in range(3):
-        for p in range(2):
-            for n in range(4):
-                values = lax.dot_general(
-                    table[f, p, :, n * width : (n + 1) * width],
-                    source[f, p],
-                    (((0,), (0,)), ((), ())),
-                    preferred_element_type=jnp.float32,
-                ).astype(jnp.bfloat16)
-                for h in range(2):
-                    for v in range(2):
-                        out[2 * (2 * n + h) + v, f, p] = values[
-                            h * half : (h + 1) * half, v * cols : (v + 1) * cols
-                        ]
+        here = slice(hop * rows, (hop + 1) * rows)
+        near = [fields[2 * band + v, 0, 0:rows, :] for v in range(2)]
+        far = [fields[2 * (7 - band) + v, 0, rows : 2 * rows, :] for v in range(2)]
+        one = jnp.concatenate(near, 1).astype(jnp.float32)
+        other = jnp.dot(flip, jnp.concatenate(far, 1), preferred_element_type=jnp.float32)
+        other = jnp.where(odd, -other, other)
+        source[0, here, :] = (one + other).astype(jnp.bfloat16)
+        source[1, here, :] = (one - other).astype(jnp.bfloat16)
+    for p in range(2):
+        for n in range(4):
+            values = lax.dot_general(
+                table[0, p, :, n * width : (n + 1) * width],
+                source[p],
+                (((0,), (0,)), ((), ())),
+                preferred_element_type=jnp.float32,
+            ).astype(jnp.bfloat16)
+            for h in range(2):
+                for v in range(2):
+                    out[2 * (2 * n + h) + v, 0, p] = values[
+                        h * half : (h + 1) * half, v * cols : (v + 1) * cols
+                    ]
 
 
 def pick_kernel(order, arrived, out):
-    for n, slot in enumerate(order):
-        out[n // 3, n % 3] = arrived[slot]
+    part = len(order) // 4
+    for quarter in range(4):
+
+        @pl.when(pl.program_id(0) == quarter)
+        def _():
+            for n in range(part):
+                out[n // 3, n % 3] = arrived[order[quarter * part + n]]
 
 
 def spread_kernel(place, lowest, owned, out):
@@ -247,10 +241,11 @@
         order += [m, 15 - m, 24 + m, m, 15 - m, 16 + m]
     handled = pl.pallas_call(
         functools.partial(pick_kernel, order),
-        in_specs=[vmem],
-        out_specs=vmem,
-        out_shape=jax.ShapeDtypeStruct((2 * bands, 3, row_count, cols), jnp.bfloat16),
-        compiler_params=roomy,
+        grid=(4,),
+        in_specs=[pl.BlockSpec((slot_count, row_count, cols), lambda n: (0, 0, 0))],
+        out_specs=pl.BlockSpec((bands // 2, 3, row_count, cols), lambda n: (n, 0, 0, 0)),
+        out_shape=shape_of(2 * bands, 3, row_count, cols),
+        compiler_params=pltpu.CompilerParams(vmem_limit_bytes=60 * 1024 * 1024),
     )(arrived)
     handled, whole, lone = lax.optimization_barrier((handled, whole, lone))
     fields = lax.all_to_all(handled, ("lat", "lev"), 0, 0, tiled=True)
@@ -272,15 +267,15 @@
     parity = jnp.take(wave_list, handling, mode="clip") % 2
     coefficients = pl.pallas_call(
         transform_kernel,
-        in_specs=[smem, any_space, any_space],
-        out_specs=vmem,
-        out_shape=jax.ShapeDtypeStruct((2 * bands, 3, 2, width // 2, cols), jnp.bfloat16),
-        scratch_shapes=[
-            pltpu.VMEM((3, 2, bands * rows, 2 * cols), jnp.bfloat16),
-            pltpu.VMEM((3, 2, bands * rows, reach), jnp.bfloat16),
-            pltpu.VMEM((2 * bands, 3, row_count, cols), jnp.bfloat16),
-            pltpu.SemaphoreType.DMA((2,)),
+        grid=(3,),
+        in_specs=[
+            smem,
+            pl.BlockSpec((1, 2, bands * rows, reach), lambda f: (f, 0, 0, 0)),
+            pl.BlockSpec((2 * bands, 1, row_count, cols), lambda f: (0, f, 0, 0)),
         ],
+        out_specs=pl.BlockSpec((2 * bands, 1, 2, width // 2, cols), lambda f: (0, f, 0, 0, 0)),
+        out_shape=shape_of(2 * bands, 3, 2, width // 2, cols),
+        scratch_shapes=[pltpu.VMEM((2, bands * rows, 2 * cols), jnp.bfloat16)],
         compiler_params=pltpu.CompilerParams(vmem_limit_bytes=60 * 1024 * 1024),
     )(jnp.concatenate([place, parity]), packed, fields)
 

time: 183 us -> 183 us (level)
  starting transfers between devices: 48.4 us -> 45.7 us
  waiting for transfers between devices: 93.4 us -> 96 us
    ppermute x10, waiting for transfers between devices: 36.8 us -> 39.6 us  [hopped(): lax.ppermute(array, 'lat', [(i, band_to(i, hop)) for i in range(bands)])]
    unnamed x30 -> x28, local copies, waits for them, and re-layouts: 9.93 us -> 8.24 us
  transfers between devices with their start and end apart: 15 -> 15, of which waited for: 5 -> 5; matrix products, arithmetic and copies ran while one was open for 2% -> 2% of each run, Pallas kernels for 6% -> 7%
where the time goes in v4:
time: 183 us; the launch traced here: 182 us
  waiting for transfers between devices  96 us (52%)
  starting transfers between devices  45.7 us (25%)
  Pallas kernels  26.3 us (14%)
  local copies, waits for them, and re-layouts  12.7 us (7%)
    ppermute x10, waiting for transfers between devices, hopped(): lax.ppermute(array, 'lat', [(i, band_to(i, hop)) for i in range(bands)])  39.6 us
    all_to_all x1, waiting for transfers between devices, shards(): fields = lax.all_to_all(handled, ('lat', 'lev'), 0, 0, tiled=True)  28 us
    all_to_all x1, waiting for transfers between devices, shards(): owned = lax.all_to_all(coefficients, ('lat', 'lev'), 0, 0, tiled=True)  21.3 us
    ppermute x10, starting transfers between devices, hopped(): lax.ppermute(array, 'lat', [(i, band_to(i, hop)) for i in range(bands)])  14.7 us
    all_to_all x1, starting transfers between devices, shards(): arrived = lax.all_to_all(outgoing, 'wave', 0, 0, tiled=True)  9.38 us
    all_to_all x1, starting transfers between devices, shards(): lax.all_to_all(listing.reshape(blocks, -1), 'wave', 0, 0, tiled=True)  9.22 us
    unnamed x28, local copies, waits for them, and re-layouts  8.24 us
    all_to_all x1, waiting for transfers between devices, shards(): lax.all_to_all(listing.reshape(blocks, -1), 'wave', 0, 0, tiled=True)  7.15 us
  transfers between devices with their start and end apart: 15, of which 5 were waited for; matrix products, arithmetic and copies ran while one was open for 2% of the time, Pallas kernels for 7%

profile of v4, /device:TPU:1, one launch (start us, length us, event | category | flops | bytes accessed | tf_op | source)
XLA Modules:
  0.0 182.2 jit_solution(8557385579643192812)
XLA Ops:
  0.0 0.0 copy-start
  0.0 0.6 pad_add_fusion.place
  0.6 0.0 copy-start.13
  0.6 3.9 %shard_map.46 = (bf16[2,128,2,512]{3,2,1,0:T(2,128)(2,1)}, bf16[2,128,2,512]{3,2,1,0:T(2,128)(2,1)}, bf16[2,128,2,512]{3,2,1,0:T(2,128)(2,1)}, bf16[6,128,2,256]{3,2,1,0:T(2,128)(2,1)}) custom-call(s32[2]{0:T(128)} %pad_add_fusion.place, bf16[32,128,2,512]{3,2,1,0:T(2,128)(2,1)} %table.3), custom_call_target="tpu_custom_call" | custom-call | tf_op jit(solution)/shard_map/pallas_call | solution.py:207
  4.5 1.3 collective-permute-start
  5.8 3.8 %collective-permute-start.1 = (bf16[2,128,2,512]{3,2,1,0:T(2,128)(2,1)}, bf16[2,128,2,512]{3,2,1,0:T(2,128)(2,1)S(1)}, u32[]{:S(2)}, u32[]{:S(2)}) collective-permute-start(bf16[2,128,2,512]{3,2,1,0:T(2,128)(2,1)} %get-tuple-element.59), channel_id=1, source_target_pairs={{0,128},{32,160},{64,192},{96,224},{128,0},{160,32},{192,64},{224,... | collective-permute-start | bytes 1572872 | tf_op jit(solution)/shard_map/ppermute | solution.py:200
  9.7 0.8 collective-permute-start.2
  10.4 0.0 collective-permute-start.3
  10.4 0.0 copy-done.13
  10.4 0.7 all_to_all.17
  11.1 9.2 %all-to-all-start = ((s32[16,1,2]{2,1,0:T(1,128)}), s32[16,1,2]{2,1,0:T(1,128)S(1)}, u32[]{:S(2)}, u32[]{:S(2)}) async-start(s32[16,1,2]{2,1,0:T(1,128)} %bitcast.3), calls=%async_computation | async-start | bytes 16384 | tf_op jit(solution)/shard_map/all_to_all | solution.py:219
  20.3 7.2 %all-to-all-done = s32[16,1,2]{2,1,0:T(1,128)S(1)} async-done(((s32[16,1,2]{2,1,0:T(1,128)}), s32[16,1,2]{2,1,0:T(1,128)S(1)}, u32[]{:S(2)}, u32[]{:S(2)}) %all-to-all-start) | async-done | bytes 160 | tf_op jit(solution)/shard_map/all_to_all | solution.py:219
  27.5 0.1 copy.10
  27.6 0.0 collective-permute-done.cross
  27.6 0.0 copy-done.2
  27.6 4.2 %shard_map.47 = (bf16[128,2,512]{2,1,0:T(2,128)(2,1)S(1)}, bf16[128,2,512]{2,1,0:T(2,128)(2,1)}, bf16[128,2,512]{2,1,0:T(2,128)(2,1)S(1)}, bf16[3,128,2,512]{3,2...) custom-call(s32[2]{0:T(128)S(1)} %copy-done.2, ...), custom_call_target="tpu_custom_call" | custom-call | flops 1000000000 | bytes 1048576 | tf_op jit(solution)/shard_map/pallas_call | solution.py:221
  31.8 0.0 copy-start.3
  31.8 0.9 copy-done.3
  32.6 0.7 copy-done.9
  33.3 0.7 copy-done.11
  34.1 0.1 copy.11
  34.1 0.1 reshape.22
  34.3 0.0 copy-done
  34.3 2.1 %gather_fusion.1 = bf16[32,256,128]{2,1,0:T(8,128)(2,1)} fusion(bf16[32,256,128]{2,1,0:T(8,128)(2,1)S(1)} %copy-done, s32[1024]{0:T(1024)S(1)} %pad_clamp_fusion), kind=kCustom, calls=%fused_computation.1 | custom fusion | bytes 4194432 | tf_op jit(solution)/shard_map/jit(_take)/gather | solution.py:232
  36.4 0.0 collective-permute-done.1.refs_0_
  36.4 0.0 collective-permute-done.2.refs_1_
  36.4 0.0 collective-permute-done.3.refs_2_
  36.4 9.4 %all-to-all-start.1 = ((bf16[32,256,128]{2,1,0:T(8,128)(2,1)}), bf16[32,256,128]{2,1,0:T(8,128)(2,1)}, u32[]{:S(2)}, u32[]{:S(2)}) async-start(bf16[32,256,128]{2,1,0:T(8,128)(2,1)} %gather_fusion.1), calls=%async_computation.1 | async-start | bytes 4194304 | tf_op jit(solution)/shard_map/all_to_all | solution.py:234
  45.8 0.0 copy-done.12
  45.8 1.3 collective-permute-start.10
  47.1 3.8 %collective-permute-start.4 = (bf16[3,128,2,512]{3,2,1,0:T(2,128)(2,1)}, bf16[3,128,2,512]{3,2,1,0:T(2,128)(2,1)}, u32[]{:S(2)}, u32[]{:S(2)}) collective-permute-start(bf16[3,128,2,512]{3,2,1,0:T(2,128)(2,1)} %get-tuple-element.67), channel_id=1, source_target_pairs={{0,160},{32,128},{64,224},{96,192},{128,32},{160,0},{192,96},{224,... | collective-permute-start | bytes 2359304 | tf_op jit(solution)/shard_map/ppermute | solution.py:200
  50.9 0.0 collective-permute-start.5
  50.9 1.7 collective-permute-start.6
  52.6 1.0 collective-permute-start.7
  53.6 0.0 collective-permute-done.10.refs_5_
  53.6 0.7 copy-done.5
  54.3 0.0 copy-done.10
  54.3 1.6 collective-permute-start.8
  56.0 37.4 %collective-permute-done.8.refs_3_ = bf16[128,2,512]{2,1,0:T(2,128)(2,1)S(1)} collective-permute-done((bf16[128,2,512]{2,1,0:T(2,128)(2,1)S(1)}, bf16[128,2,512]{2,1,0:T(2,128)(2,1)S(1)}, u32[]{:S(2)}, u32[]{:S(2)}) %collective-permute-start.8) | collective-permute-done | bytes 262176 | tf_op jit(solution)/shard_map/ppermute | solution.py:200
  93.4 0.7 copy-done.7
  94.1 0.7 collective-permute-start.9
  94.8 0.0 all-to-all-done.1.arrived
  94.8 3.9 %shard_map.48 = bf16[16,3,256,128]{3,2,1,0:T(8,128)(2,1)} custom-call(bf16[32,256,128]{2,1,0:T(8,128)(2,1)} %all-to-all-done.1.arrived), custom_call_target="tpu_custom_call" | custom-call | tf_op jit(solution)/shard_map/pallas_call | solution.py:242
  98.7 2.2 %collective-permute-done.9.refs_4_ = bf16[128,2,512]{2,1,0:T(2,128)(2,1)} collective-permute-done((bf16[128,2,512]{2,1,0:T(2,128)(2,1)}, bf16[128,2,512]{2,1,0:T(2,128)(2,1)}, u32[]{:S(2)}, u32[]{:S(2)}) %collective-permute-start.9) | collective-permute-done | bytes 262176 | tf_op jit(solution)/shard_map/ppermute | solution.py:200
  100.9 0.0 collective-permute-done.4.refs_7_
  100.9 0.0 collective-permute-done.5.refs_8_
  100.9 0.0 collective-permute-done.6.refs_9_
  100.9 0.0 collective-permute-done.7.refs_10_
  100.9 6.0 %all-to-all-start.2 = ((bf16[16,3,256,128]{3,2,1,0:T(8,128)(2,1)}), bf16[16,3,256,128]{3,2,1,0:T(8,128)(2,1)}, u32[]{:S(2)}, u32[]{:S(2)}) async-start(bf16[16,3,256,128]{3,2,1,0:T(8,128)(2,1)} %shard_map.48), calls=%async_computation.2 | async-start | bytes 6291456 | tf_op jit(solution)/shard_map/all_to_all | solution.py:251
  106.9 0.7 dynamic-slice_bitcast_fusion
  107.6 0.6 gather_fusion
  108.3 0.7 pad_add_fusion.1.place
  108.9 0.0 copy-done.4
  108.9 0.9 copy-done.6
  109.9 0.9 copy-done.8
  110.8 4.1 %shard_map.49.table = bf16[3,2,1024,512]{3,2,1,0:T(8,128)(2,1)S(1)} custom-call(bf16[2,128,2,512]{3,2,1,0:T(2,128)(2,1)S(1)} %collective-permute-done.1.refs_0_, bf16[2,128,2,512]{3,2,1,0:T(2,128)(2,1)} %collective-permute-done.2.refs_1_, bf16[2,128,2,512]{3,2,1,0:T(2,128)(2,1)} %collective-permute-done.3.refs_2_, bf16[128,2,512]{2,1,0:T(2,128)(2,1)S(1)} %copy-done.8, ...), custom_call_target="tpu_custom_call" | custom-call | flops 20000000000 | bytes 25165824 | tf_op jit(solution)/shard_map/pallas_call | solution.py:253
  114.9 0.0 copy-start.1
  114.9 2.6 %copy-done.1 = bf16[3,2,1024,512]{3,2,1,0:T(8,128)(2,1)} copy-done((bf16[3,2,1024,512]{3,2,1,0:T(8,128)(2,1)}, bf16[3,2,1024,512]{3,2,1,0:T(8,128)(2,1)S(1)}, u32[]{:S(2)}) %copy-start.1) | copy-done | bytes 6291480
  117.6 28.0 %all-to-all-done.2.fields = bf16[16,3,256,128]{3,2,1,0:T(8,128)(2,1)} async-done(((bf16[16,3,256,128]{3,2,1,0:T(8,128)(2,1)}), bf16[16,3,256,128]{3,2,1,0:T(8,128)(2,1)}, u32[]{:S(2)}, u32[]{:S(2)}) %all-to-all-start.2) | async-done | bytes 3145760 | tf_op jit(solution)/shard_map/all_to_all | solution.py:251
  145.5 7.0 %shard_map.50 = bf16[16,3,2,64,128]{4,3,2,1,0:T(8,128)(2,1)} custom-call(s32[5]{0:T(128)} %pad_add_fusion.1.place, bf16[3,2,1024,512]{3,2,1,0:T(8,128)(2,1)} %copy-done.1, bf16[16,3,256,128]{3,2,1,0:T(8,128)(2,1)} %all-to-all-done.2.fields), custom_call_target="tpu_custom_call" | custom-call | tf_op jit(solution)/shard_map/pallas_call | solution.py:268
  152.5 5.1 %all-to-all-start.3 = ((bf16[16,3,2,64,128]{4,3,2,1,0:T(8,128)(2,1)}), bf16[16,3,2,64,128]{4,3,2,1,0:T(8,128)(2,1)}, u32[]{:S(2)}, u32[]{:S(2)}) async-start(bf16[16,3,2,64,128]{4,3,2,1,0:T(8,128)(2,1)} %shard_map.50), calls=%async_computation.3 | async-start | bytes 3145728 | tf_op jit(solution)/shard_map/all_to_all | solution.py:282
  157.6 21.3 %all-to-all-done.3.owned = bf16[16,3,2,64,128]{4,3,2,1,0:T(8,128)(2,1)} async-done(((bf16[16,3,2,64,128]{4,3,2,1,0:T(8,128)(2,1)}), bf16[16,3,2,64,128]{4,3,2,1,0:T(8,128)(2,1)}, u32[]{:S(2)}, u32[]{:S(2)}) %all-to-all-start.3) | async-done | bytes 1572896 | tf_op jit(solution)/shard_map/all_to_all | solution.py:282
  178.8 0.1 broadcast_in_dim.14.lowest
  178.9 3.3 %shard_map.51 = bf16[2,64,2,32,128]{4,3,2,1,0:T(8,128)(2,1)} custom-call(s32[2]{0:T(128)S(1)} %copy-done.2, s32[32,128]{1,0:T(8,128)S(1)} %broadcast_in_dim.14.lowest, bf16[16,3,2,64,128]{4,3,2,1,0:T(8,128)(2,1)} %all-to-all-done.3.owned), custom_call_target="tpu_custom_call" | custom-call | tf_op jit(solution)/shard_map/pallas_call | solution.py:286
  (15 shorter events, 0.1 us)
Async XLA Ops:
  0.0 34.3 %copy-start = (bf16[32,256,128]{2,1,0:T(8,128)(2,1)S(1)}, bf16[32,256,128]{2,1,0:T(8,128)(2,1)}, u32[]{:S(2)}) copy-start(bf16[32,256,128]{2,1,0:T(8,128)(2,1)} %param.4) | copy-start | bytes 6291460
  0.6 9.8 %copy-start.13 = (s32[32]{0:T(128)S(1)}, s32[32]{0:T(128)}, u32[]{:S(2)}) copy-start(s32[32]{0:T(128)} %param.6) | copy-start | bytes 388
  0.6 26.9 %copy-start.2 = (s32[2]{0:T(128)S(1)}, s32[2]{0:T(128)}, u32[]{:S(2)}) copy-start(s32[2]{0:T(128)} %pad_add_fusion.place) | copy-start | bytes 28
  4.5 23.1 %collective-permute-start = (bf16[6,128,2,256]{3,2,1,0:T(2,128)(2,1)}, bf16[6,128,2,256]{3,2,1,0:T(2,128)(2,1)S(1)}, u32[]{:S(2)}, u32[]{:S(2)}) collective-permute-start(bf16[6,128,2,256]{3,2,1,0:T(2,128)(2,1)} %get-tuple-element.49), channel_id=1, source_target_pairs={{1,0},{3,2},{5,4},{7,6},{9,8},{11,10},{13,12},{15,14},{17,16},{19,... | collective-permute-start | bytes 2359304 | tf_op jit(solution)/shard_map/ppermute | solution.py:216
  5.8 30.6 %collective-permute-start.1 = (bf16[2,128,2,512]{3,2,1,0:T(2,128)(2,1)}, bf16[2,128,2,512]{3,2,1,0:T(2,128)(2,1)S(1)}, u32[]{:S(2)}, u32[]{:S(2)}) collective-permute-start(bf16[2,128,2,512]{3,2,1,0:T(2,128)(2,1)} %get-tuple-element.59), channel_id=1, source_target_pairs={{0,128},{32,160},{64,192},{96,224},{128,0},{160,32},{192,64},{224,... | collective-permute-start | bytes 1572872 | tf_op jit(solution)/shard_map/ppermute | solution.py:200
  9.7 26.8 %collective-permute-start.2 = (bf16[2,128,2,512]{3,2,1,0:T(2,128)(2,1)}, bf16[2,128,2,512]{3,2,1,0:T(2,128)(2,1)}, u32[]{:S(2)}, u32[]{:S(2)}) collective-permute-start(bf16[2,128,2,512]{3,2,1,0:T(2,128)(2,1)} %get-tuple-element.60), channel_id=1, source_target_pairs={{0,64},{32,224},{64,0},{96,160},{128,192},{160,96},{192,128},{224,... | collective-permute-start | bytes 1572872 | tf_op jit(solution)/shard_map/ppermute | solution.py:200
  10.4 26.0 %collective-permute-start.3 = (bf16[2,128,2,512]{3,2,1,0:T(2,128)(2,1)}, bf16[2,128,2,512]{3,2,1,0:T(2,128)(2,1)}, u32[]{:S(2)}, u32[]{:S(2)}) collective-permute-start(bf16[2,128,2,512]{3,2,1,0:T(2,128)(2,1)} %get-tuple-element.61), channel_id=1, source_target_pairs={{0,192},{32,96},{64,128},{96,32},{128,64},{160,224},{192,0},{224,1... | collective-permute-start | bytes 1572872 | tf_op jit(solution)/shard_map/ppermute | solution.py:200
  11.1 16.4 %all-to-all-start = ((s32[16,1,2]{2,1,0:T(1,128)}), s32[16,1,2]{2,1,0:T(1,128)S(1)}, u32[]{:S(2)}, u32[]{:S(2)}) async-start(s32[16,1,2]{2,1,0:T(1,128)} %bitcast.3), calls=%async_computation | async-start | bytes 16384 | tf_op jit(solution)/shard_map/all_to_all | solution.py:219
  31.8 0.9 copy-start.3
  32.6 0.7 copy-start.9
  33.3 0.7 copy-start.11
  36.4 9.4 %copy-start.12 = (bf16[128,2,512]{2,1,0:T(2,128)(2,1)S(1)}, bf16[128,2,512]{2,1,0:T(2,128)(2,1)}, u32[]{:S(2)}) copy-start(bf16[128,2,512]{2,1,0:T(2,128)(2,1)} %copy-done.11) | copy-start | bytes 786436
  36.4 17.9 %copy-start.10 = (bf16[128,2,512]{2,1,0:T(2,128)(2,1)S(1)}, bf16[128,2,512]{2,1,0:T(2,128)(2,1)}, u32[]{:S(2)}) copy-start(bf16[128,2,512]{2,1,0:T(2,128)(2,1)} %copy-done.9) | copy-start | bytes 786436
  36.4 58.3 %all-to-all-start.1 = ((bf16[32,256,128]{2,1,0:T(8,128)(2,1)}), bf16[32,256,128]{2,1,0:T(8,128)(2,1)}, u32[]{:S(2)}, u32[]{:S(2)}) async-start(bf16[32,256,128]{2,1,0:T(8,128)(2,1)} %gather_fusion.1), calls=%async_computation.1 | async-start | bytes 4194304 | tf_op jit(solution)/shard_map/all_to_all | solution.py:234
  45.8 7.8 %collective-permute-start.10 = (bf16[128,2,512]{2,1,0:T(2,128)(2,1)S(1)}, bf16[128,2,512]{2,1,0:T(2,128)(2,1)S(1)}, u32[]{:S(2)}, u32[]{:S(2)}) collective-permute-start(bf16[128,2,512]{2,1,0:T(2,128)(2,1)S(1)} %copy-done.12), channel_id=1, source_target_pairs={{0,192},{32,96},{64,128},{96,32},{128,64},{160,224},{192,0},{224,1... | collective-permute-start | bytes 786440 | tf_op jit(solution)/shard_map/ppermute | solution.py:200
  47.1 53.8 %collective-permute-start.4 = (bf16[3,128,2,512]{3,2,1,0:T(2,128)(2,1)}, bf16[3,128,2,512]{3,2,1,0:T(2,128)(2,1)}, u32[]{:S(2)}, u32[]{:S(2)}) collective-permute-start(bf16[3,128,2,512]{3,2,1,0:T(2,128)(2,1)} %get-tuple-element.67), channel_id=1, source_target_pairs={{0,160},{32,128},{64,224},{96,192},{128,32},{160,0},{192,96},{224,... | collective-permute-start | bytes 2359304 | tf_op jit(solution)/shard_map/ppermute | solution.py:200
  50.9 50.0 %collective-permute-start.5 = (bf16[3,128,2,512]{3,2,1,0:T(2,128)(2,1)}, bf16[3,128,2,512]{3,2,1,0:T(2,128)(2,1)}, u32[]{:S(2)}, u32[]{:S(2)}) collective-permute-start(bf16[3,128,2,512]{3,2,1,0:T(2,128)(2,1)} %get-tuple-element.68), channel_id=1, source_target_pairs={{0,96},{32,192},{64,32},{96,128},{128,224},{160,64},{192,160},{224... | collective-permute-start | bytes 2359304 | tf_op jit(solution)/shard_map/ppermute | solution.py:200
  50.9 50.0 %collective-permute-start.6 = (bf16[3,128,2,512]{3,2,1,0:T(2,128)(2,1)}, bf16[3,128,2,512]{3,2,1,0:T(2,128)(2,1)}, u32[]{:S(2)}, u32[]{:S(2)}) collective-permute-start(bf16[3,128,2,512]{3,2,1,0:T(2,128)(2,1)} %get-tuple-element.69), channel_id=1, source_target_pairs={{0,224},{32,64},{64,160},{96,0},{128,96},{160,192},{192,32},{224,1... | collective-permute-start | bytes 2359304 | tf_op jit(solution)/shard_map/ppermute | solution.py:200
  52.6 48.2 %collective-permute-start.7 = (bf16[3,128,2,512]{3,2,1,0:T(2,128)(2,1)}, bf16[3,128,2,512]{3,2,1,0:T(2,128)(2,1)}, u32[]{:S(2)}, u32[]{:S(2)}) collective-permute-start(bf16[3,128,2,512]{3,2,1,0:T(2,128)(2,1)} %get-tuple-element.70), channel_id=1, source_target_pairs={{0,32},{32,0},{64,96},{96,64},{128,160},{160,128},{192,224},{224,1... | collective-permute-start | bytes 2359304 | tf_op jit(solution)/shard_map/ppermute | solution.py:200
  53.6 0.7 copy-start.5
  54.3 39.1 %collective-permute-start.8 = (bf16[128,2,512]{2,1,0:T(2,128)(2,1)S(1)}, bf16[128,2,512]{2,1,0:T(2,128)(2,1)S(1)}, u32[]{:S(2)}, u32[]{:S(2)}) collective-permute-start(bf16[128,2,512]{2,1,0:T(2,128)(2,1)S(1)} %copy-done.10), channel_id=1, source_target_pairs={{0,128},{32,160},{64,192},{96,224},{128,0},{160,32},{192,64},{224,... | collective-permute-start | bytes 786440 | tf_op jit(solution)/shard_map/ppermute | solution.py:200
  93.4 0.7 copy-start.7
  94.1 6.7 %collective-permute-start.9 = (bf16[128,2,512]{2,1,0:T(2,128)(2,1)}, bf16[128,2,512]{2,1,0:T(2,128)(2,1)}, u32[]{:S(2)}, u32[]{:S(2)}) collective-permute-start(bf16[128,2,512]{2,1,0:T(2,128)(2,1)} %get-tuple-element.72), channel_id=1, source_target_pairs={{0,64},{32,224},{64,0},{96,160},{128,192},{160,96},{192,128},{224,... | collective-permute-start | bytes 786440 | tf_op jit(solution)/shard_map/ppermute | solution.py:200
  98.7 10.3 %copy-start.4 = (bf16[3,128,2,512]{3,2,1,0:T(2,128)(2,1)S(1)}, bf16[3,128,2,512]{3,2,1,0:T(2,128)(2,1)}, u32[]{:S(2)}) copy-start(bf16[3,128,2,512]{3,2,1,0:T(2,128)(2,1)} %copy-done.3) | copy-start | bytes 2359300
  100.9 44.6 %all-to-all-start.2 = ((bf16[16,3,256,128]{3,2,1,0:T(8,128)(2,1)}), bf16[16,3,256,128]{3,2,1,0:T(8,128)(2,1)}, u32[]{:S(2)}, u32[]{:S(2)}) async-start(bf16[16,3,256,128]{3,2,1,0:T(8,128)(2,1)} %shard_map.48), calls=%async_computation.2 | async-start | bytes 6291456 | tf_op jit(solution)/shard_map/all_to_all | solution.py:251
  108.9 1.0 copy-start.6
  109.9 0.9 copy-start.8
  114.9 2.6 %copy-start.1 = (bf16[3,2,1024,512]{3,2,1,0:T(8,128)(2,1)}, bf16[3,2,1024,512]{3,2,1,0:T(8,128)(2,1)S(1)}, u32[]{:S(2)}) copy-start(bf16[3,2,1024,512]{3,2,1,0:T(8,128)(2,1)S(1)} %shard_map.49.table) | copy-start | bytes 18874372
  152.5 26.3 %all-to-all-start.3 = ((bf16[16,3,2,64,128]{4,3,2,1,0:T(8,128)(2,1)}), bf16[16,3,2,64,128]{4,3,2,1,0:T(8,128)(2,1)}, u32[]{:S(2)}, u32[]{:S(2)}) async-start(bf16[16,3,2,64,128]{4,3,2,1,0:T(8,128)(2,1)} %shard_map.50), calls=%async_computation.3 | async-start | bytes 3145728 | tf_op jit(solution)/shard_map/all_to_all | solution.py:282

commit v5 on v4

--- a/solution.py
+++ b/solution.py
@@ -218,6 +218,10 @@
 
     wanted = lax.all_to_all(listing.reshape(blocks, -1), "wave", 0, 0, tiled=True)
 
+    local = (wanted - block_id * slot_count).reshape(-1)
+    outgoing = jnp.take(fourier, local, axis=0, mode="clip")
+    outgoing, cross, first[:2] = lax.optimization_barrier((outgoing, cross, first[:2]))
+    arrived = lax.all_to_all(outgoing, "wave", 0, 0, tiled=True)
     rest = pl.pallas_call(
         rest_kernel,
         in_specs=[smem, any_space, vmem],
@@ -227,11 +231,6 @@
         compiler_params=pltpu.CompilerParams(vmem_limit_bytes=48 * 1024 * 1024),
         cost_estimate=pl.CostEstimate(flops=10**9, bytes_accessed=2**20, transcendentals=0),
     )(place, legendre, cross)
-    wanted, rest = lax.optimization_barrier((wanted, rest))
-    local = (wanted - block_id * slot_count).reshape(-1)
-    outgoing = jnp.take(fourier, local, axis=0, mode="clip")
-    outgoing, first = lax.optimization_barrier((outgoing, first))
-    arrived = lax.all_to_all(outgoing, "wave", 0, 0, tiled=True)
     lone, (mine, *whole) = rest[:3], rest[3:]
     whole = [mine] + [hopped(array, hop) for array, hop in zip(whole, LAST)]
     lone = [hopped(array, hop) for array, hop in zip(lone, FIRST)]
@@ -247,7 +246,7 @@
         out_shape=shape_of(2 * bands, 3, row_count, cols),
         compiler_params=pltpu.CompilerParams(vmem_limit_bytes=60 * 1024 * 1024),
     )(arrived)
-    handled, whole, lone = lax.optimization_barrier((handled, whole, lone))
+    handled, first, whole, lone = lax.optimization_barrier((handled, first, whole, lone))
     fields = lax.all_to_all(handled, ("lat", "lev"), 0, 0, tiled=True)
 
     packed = pl.pallas_call(

time: 183 us -> 182 us (level)
  waiting for transfers between devices: 96 us -> 93.1 us
  local copies, waits for them, and re-layouts: 12.7 us -> 15 us
    unnamed x28, local copies, waits for them, and re-layouts: 8.24 us -> 10.7 us
    all_to_all x1, starting transfers between devices: 9.38 us -> 7.26 us  [shards(): arrived = lax.all_to_all(outgoing, 'wave', 0, 0, tiled=True)]
where the time goes in v5:
time: 182 us; the launch traced here: 181 us
  waiting for transfers between devices  93.1 us (51%)
  starting transfers between devices  45.5 us (25%)
  Pallas kernels  25.9 us (14%)
  local copies, waits for them, and re-layouts  15 us (8%)
    ppermute x10, waiting for transfers between devices, hopped(): lax.ppermute(array, 'lat', [(i, band_to(i, hop)) for i in range(bands)])  38.4 us
    all_to_all x1, waiting for transfers between devices, shards(): fields = lax.all_to_all(handled, ('lat', 'lev'), 0, 0, tiled=True)  26.2 us
    all_to_all x1, waiting for transfers between devices, shards(): owned = lax.all_to_all(coefficients, ('lat', 'lev'), 0, 0, tiled=True)  21.3 us
    ppermute x10, starting transfers between devices, hopped(): lax.ppermute(array, 'lat', [(i, band_to(i, hop)) for i in range(bands)])  15.5 us
    unnamed x28, local copies, waits for them, and re-layouts  10.7 us
    all_to_all x1, starting transfers between devices, shards(): lax.all_to_all(listing.reshape(blocks, -1), 'wave', 0, 0, tiled=True)  9.22 us
    all_to_all x1, starting transfers between devices, shards(): arrived = lax.all_to_all(outgoing, 'wave', 0, 0, tiled=True)  7.26 us
    all_to_all x1, waiting for transfers between devices, shards(): lax.all_to_all(listing.reshape(blocks, -1), 'wave', 0, 0, tiled=True)  7.22 us
  transfers between devices with their start and end apart: 15, of which 5 were waited for; matrix products, arithmetic and copies ran while one was open for 2% of the time, Pallas kernels for 7%

profile of v5, /device:TPU:1, one launch (start us, length us, event | category | flops | bytes accessed | tf_op | source)
XLA Modules:
  0.0 181.0 jit_solution(11917681922394359043)
XLA Ops:
  0.0 0.0 copy-start
  0.0 0.6 pad_add_fusion.place
  0.6 3.9 %shard_map.46 = (bf16[2,128,2,512]{3,2,1,0:T(2,128)(2,1)}, bf16[2,128,2,512]{3,2,1,0:T(2,128)(2,1)}, bf16[2,128,2,512]{3,2,1,0:T(2,128)(2,1)}, bf16[6,128,2,256]{3,2,1,0:T(2,128)(2,1)}) custom-call(s32[2]{0:T(128)} %pad_add_fusion.place, bf16[32,128,2,512]{3,2,1,0:T(2,128)(2,1)} %table.3), custom_call_target="tpu_custom_call" | custom-call | tf_op jit(solution)/shard_map/pallas_call | solution.py:207
  4.5 1.3 collective-permute-start
  5.8 3.8 %collective-permute-start.1 = (bf16[2,128,2,512]{3,2,1,0:T(2,128)(2,1)}, bf16[2,128,2,512]{3,2,1,0:T(2,128)(2,1)S(1)}, u32[]{:S(2)}, u32[]{:S(2)}) collective-permute-start(bf16[2,128,2,512]{3,2,1,0:T(2,128)(2,1)} %get-tuple-element.44), channel_id=1, source_target_pairs={{0,128},{32,160},{64,192},{96,224},{128,0},{160,32},{192,64},{224,... | collective-permute-start | bytes 1572872 | tf_op jit(solution)/shard_map/ppermute | solution.py:200
  9.6 0.8 collective-permute-start.2
  10.4 0.0 copy-done.13
  10.4 0.7 all_to_all.15
  11.1 9.2 %all-to-all-start = ((s32[16,1,2]{2,1,0:T(1,128)}), s32[16,1,2]{2,1,0:T(1,128)S(1)}, u32[]{:S(2)}, u32[]{:S(2)}) async-start(s32[16,1,2]{2,1,0:T(1,128)} %bitcast.3), calls=%async_computation | async-start | bytes 16384 | tf_op jit(solution)/shard_map/all_to_all | solution.py:219
  20.3 7.2 %all-to-all-done = s32[16,1,2]{2,1,0:T(1,128)S(1)} async-done(((s32[16,1,2]{2,1,0:T(1,128)}), s32[16,1,2]{2,1,0:T(1,128)S(1)}, u32[]{:S(2)}, u32[]{:S(2)}) %all-to-all-start) | async-done | bytes 160 | tf_op jit(solution)/shard_map/all_to_all | solution.py:219
  27.6 0.1 reshape.34
  27.7 0.0 copy-done
  27.7 2.1 %gather_fusion.1 = bf16[32,256,128]{2,1,0:T(8,128)(2,1)} fusion(bf16[32,256,128]{2,1,0:T(8,128)(2,1)S(1)} %copy-done, s32[1024]{0:T(1024)S(1)} %pad_clamp_fusion), kind=kCustom, calls=%fused_computation.1 | custom fusion | bytes 4194432 | tf_op jit(solution)/shard_map/jit(_take)/gather | solution.py:222
  29.8 0.0 copy-start.2
  29.8 0.0 collective-permute-done.1.refs_0_
  29.8 0.0 collective-permute-done.2.refs_1_
  29.8 0.0 collective-permute-done.cross
  29.8 7.3 %all-to-all-start.1 = ((bf16[32,256,128]{2,1,0:T(8,128)(2,1)}), bf16[32,256,128]{2,1,0:T(8,128)(2,1)}, u32[]{:S(2)}, u32[]{:S(2)}) async-start(bf16[32,256,128]{2,1,0:T(8,128)(2,1)} %gather_fusion.1), calls=%async_computation.1 | async-start | bytes 4194304 | tf_op jit(solution)/shard_map/all_to_all | solution.py:224
  37.1 1.6 collective-permute-start.3
  38.7 0.0 copy-done.2
  38.7 4.2 %shard_map.48 = (bf16[128,2,512]{2,1,0:T(2,128)(2,1)S(1)}, bf16[128,2,512]{2,1,0:T(2,128)(2,1)}, bf16[128,2,512]{2,1,0:T(2,128)(2,1)S(1)}, bf16[3,128,2,512]{3,2...) custom-call(s32[2]{0:T(128)S(1)} %copy-done.2, ...), custom_call_target="tpu_custom_call" | custom-call | flops 1000000000 | bytes 1048576 | tf_op jit(solution)/shard_map/pallas_call | solution.py:225
  42.9 0.0 copy-start.3
  42.9 0.9 copy-done.3
  43.8 0.0 collective-permute-start.10
  43.9 4.7 %collective-permute-start.4 = (bf16[3,128,2,512]{3,2,1,0:T(2,128)(2,1)}, bf16[3,128,2,512]{3,2,1,0:T(2,128)(2,1)S(1)}, u32[]{:S(2)}, u32[]{:S(2)}) collective-permute-start(bf16[3,128,2,512]{3,2,1,0:T(2,128)(2,1)} %get-tuple-element.52), channel_id=1, source_target_pairs={{0,160},{32,128},{64,224},{96,192},{128,32},{160,0},{192,96},{224,... | collective-permute-start | bytes 2359304 | tf_op jit(solution)/shard_map/ppermute | solution.py:200
  48.5 1.0 collective-permute-start.5
  49.6 0.7 collective-permute-start.6
  50.3 0.0 collective-permute-done.3.refs_2_
  50.3 0.0 copy-start.7
  50.3 0.8 copy-done.7
  51.1 0.3 collective-permute-start.7
  51.3 0.0 collective-permute-done.10.refs_5_
  51.3 0.7 copy-done.9
  52.0 1.8 collective-permute-start.8
  53.8 36.3 %collective-permute-done.8.refs_3_ = bf16[128,2,512]{2,1,0:T(2,128)(2,1)S(1)} collective-permute-done((bf16[128,2,512]{2,1,0:T(2,128)(2,1)S(1)}, bf16[128,2,512]{2,1,0:T(2,128)(2,1)S(1)}, u32[]{:S(2)}, u32[]{:S(2)}) %collective-permute-start.8) | collective-permute-done | bytes 262176 | tf_op jit(solution)/shard_map/ppermute | solution.py:200
  90.2 0.7 copy-done.11
  90.9 0.8 collective-permute-start.9
  91.6 0.0 all-to-all-done.1.arrived
  91.6 3.9 %shard_map.47 = bf16[16,3,256,128]{3,2,1,0:T(8,128)(2,1)} custom-call(bf16[32,256,128]{2,1,0:T(8,128)(2,1)} %all-to-all-done.1.arrived), custom_call_target="tpu_custom_call" | custom-call | tf_op jit(solution)/shard_map/pallas_call | solution.py:241
  95.5 2.1 %collective-permute-done.9.refs_4_ = bf16[128,2,512]{2,1,0:T(2,128)(2,1)} collective-permute-done((bf16[128,2,512]{2,1,0:T(2,128)(2,1)}, bf16[128,2,512]{2,1,0:T(2,128)(2,1)}, u32[]{:S(2)}, u32[]{:S(2)}) %collective-permute-start.9) | collective-permute-done | bytes 262176 | tf_op jit(solution)/shard_map/ppermute | solution.py:200
  97.6 0.0 collective-permute-done.4.refs_7_
  97.6 0.9 copy-done.5
  98.5 0.0 collective-permute-done.5.refs_8_
  98.5 0.0 collective-permute-done.6.refs_9_
  98.5 0.0 collective-permute-done.7.refs_10_
  98.5 0.0 copy-start.4
  98.5 7.2 %all-to-all-start.2 = ((bf16[16,3,256,128]{3,2,1,0:T(8,128)(2,1)}), bf16[16,3,256,128]{3,2,1,0:T(8,128)(2,1)}, u32[]{:S(2)}, u32[]{:S(2)}) async-start(bf16[16,3,256,128]{3,2,1,0:T(8,128)(2,1)} %shard_map.47), calls=%async_computation.2 | async-start | bytes 6291456 | tf_op jit(solution)/shard_map/all_to_all | solution.py:250
  105.7 0.7 dynamic-slice_bitcast_fusion
  106.4 0.6 gather_fusion
  107.1 0.7 pad_add_fusion.1.place
  107.7 0.0 copy-done.4
  107.7 1.1 copy-done.6
  108.9 1.0 copy-done.8
  109.9 0.9 copy-done.10
  110.9 0.9 copy-done.12
  111.8 3.7 %shard_map.49.table = bf16[3,2,1024,512]{3,2,1,0:T(8,128)(2,1)S(1)} custom-call(bf16[2,128,2,512]{3,2,1,0:T(2,128)(2,1)S(1)} %collective-permute-done.1.refs_0_, bf16[2,128,2,512]{3,2,1,0:T(2,128)(2,1)} %collective-permute-done.2.refs_1_, bf16[2,128,2,512]{3,2,1,0:T(2,128)(2,1)S(1)} %copy-done.8, bf16[128,2,512]{2,1,0:T(2,128)(2,1)S(1)} %copy-done.12, ...), custom_call_target="tpu_custom_call" | custom-call | flops 20000000000 | bytes 25165824 | tf_op jit(solution)/shard_map/pallas_call | solution.py:252
  115.5 0.0 copy-start.1
  115.5 2.6 %copy-done.1 = bf16[3,2,1024,512]{3,2,1,0:T(8,128)(2,1)} copy-done((bf16[3,2,1024,512]{3,2,1,0:T(8,128)(2,1)}, bf16[3,2,1024,512]{3,2,1,0:T(8,128)(2,1)S(1)}, u32[]{:S(2)}) %copy-start.1) | copy-done | bytes 6291480
  118.1 26.2 %all-to-all-done.2.fields = bf16[16,3,256,128]{3,2,1,0:T(8,128)(2,1)} async-done(((bf16[16,3,256,128]{3,2,1,0:T(8,128)(2,1)}), bf16[16,3,256,128]{3,2,1,0:T(8,128)(2,1)}, u32[]{:S(2)}, u32[]{:S(2)}) %all-to-all-start.2) | async-done | bytes 3145760 | tf_op jit(solution)/shard_map/all_to_all | solution.py:250
  144.3 6.9 %shard_map.50 = bf16[16,3,2,64,128]{4,3,2,1,0:T(8,128)(2,1)} custom-call(s32[5]{0:T(128)} %pad_add_fusion.1.place, bf16[3,2,1024,512]{3,2,1,0:T(8,128)(2,1)} %copy-done.1, bf16[16,3,256,128]{3,2,1,0:T(8,128)(2,1)} %all-to-all-done.2.fields), custom_call_target="tpu_custom_call" | custom-call | tf_op jit(solution)/shard_map/pallas_call | solution.py:267
  151.3 5.1 %all-to-all-start.3 = ((bf16[16,3,2,64,128]{4,3,2,1,0:T(8,128)(2,1)}), bf16[16,3,2,64,128]{4,3,2,1,0:T(8,128)(2,1)}, u32[]{:S(2)}, u32[]{:S(2)}) async-start(bf16[16,3,2,64,128]{4,3,2,1,0:T(8,128)(2,1)} %shard_map.50), calls=%async_computation.3 | async-start | bytes 3145728 | tf_op jit(solution)/shard_map/all_to_all | solution.py:281
  156.3 21.3 %all-to-all-done.3.owned = bf16[16,3,2,64,128]{4,3,2,1,0:T(8,128)(2,1)} async-done(((bf16[16,3,2,64,128]{4,3,2,1,0:T(8,128)(2,1)}), bf16[16,3,2,64,128]{4,3,2,1,0:T(8,128)(2,1)}, u32[]{:S(2)}, u32[]{:S(2)}) %all-to-all-start.3) | async-done | bytes 1572896 | tf_op jit(solution)/shard_map/all_to_all | solution.py:281
  177.6 0.1 broadcast_in_dim.12.lowest
  177.7 3.3 %shard_map.51 = bf16[2,64,2,32,128]{4,3,2,1,0:T(8,128)(2,1)} custom-call(s32[2]{0:T(128)S(1)} %copy-done.2, s32[32,128]{1,0:T(8,128)S(1)} %broadcast_in_dim.12.lowest, bf16[16,3,2,64,128]{4,3,2,1,0:T(8,128)(2,1)} %all-to-all-done.3.owned), custom_call_target="tpu_custom_call" | custom-call | tf_op jit(solution)/shard_map/pallas_call | solution.py:285
  (13 shorter events, 0.1 us)
Async XLA Ops:
  0.0 27.7 %copy-start = (bf16[32,256,128]{2,1,0:T(8,128)(2,1)S(1)}, bf16[32,256,128]{2,1,0:T(8,128)(2,1)}, u32[]{:S(2)}) copy-start(bf16[32,256,128]{2,1,0:T(8,128)(2,1)} %param.4) | copy-start | bytes 6291460
  0.6 9.8 %copy-start.13 = (s32[32]{0:T(128)S(1)}, s32[32]{0:T(128)}, u32[]{:S(2)}) copy-start(s32[32]{0:T(128)} %param.6) | copy-start | bytes 388
  4.5 25.3 %collective-permute-start = (bf16[6,128,2,256]{3,2,1,0:T(2,128)(2,1)}, bf16[6,128,2,256]{3,2,1,0:T(2,128)(2,1)S(1)}, u32[]{:S(2)}, u32[]{:S(2)}) collective-permute-start(bf16[6,128,2,256]{3,2,1,0:T(2,128)(2,1)} %get-tuple-element.43), channel_id=1, source_target_pairs={{1,0},{3,2},{5,4},{7,6},{9,8},{11,10},{13,12},{15,14},{17,16},{19,... | collective-permute-start | bytes 2359304 | tf_op jit(solution)/shard_map/ppermute | solution.py:216
  5.8 24.0 %collective-permute-start.1 = (bf16[2,128,2,512]{3,2,1,0:T(2,128)(2,1)}, bf16[2,128,2,512]{3,2,1,0:T(2,128)(2,1)S(1)}, u32[]{:S(2)}, u32[]{:S(2)}) collective-permute-start(bf16[2,128,2,512]{3,2,1,0:T(2,128)(2,1)} %get-tuple-element.44), channel_id=1, source_target_pairs={{0,128},{32,160},{64,192},{96,224},{128,0},{160,32},{192,64},{224,... | collective-permute-start | bytes 1572872 | tf_op jit(solution)/shard_map/ppermute | solution.py:200
  9.6 20.2 %collective-permute-start.2 = (bf16[2,128,2,512]{3,2,1,0:T(2,128)(2,1)}, bf16[2,128,2,512]{3,2,1,0:T(2,128)(2,1)}, u32[]{:S(2)}, u32[]{:S(2)}) collective-permute-start(bf16[2,128,2,512]{3,2,1,0:T(2,128)(2,1)} %get-tuple-element.45), channel_id=1, source_target_pairs={{0,64},{32,224},{64,0},{96,160},{128,192},{160,96},{192,128},{224,... | collective-permute-start | bytes 1572872 | tf_op jit(solution)/shard_map/ppermute | solution.py:200
  11.1 16.5 %all-to-all-start = ((s32[16,1,2]{2,1,0:T(1,128)}), s32[16,1,2]{2,1,0:T(1,128)S(1)}, u32[]{:S(2)}, u32[]{:S(2)}) async-start(s32[16,1,2]{2,1,0:T(1,128)} %bitcast.3), calls=%async_computation | async-start | bytes 16384 | tf_op jit(solution)/shard_map/all_to_all | solution.py:219
  29.8 8.9 %copy-start.2 = (s32[2]{0:T(128)S(1)}, s32[2]{0:T(128)}, u32[]{:S(2)}) copy-start(s32[2]{0:T(128)} %pad_add_fusion.place) | copy-start | bytes 28
  29.8 61.8 %all-to-all-start.1 = ((bf16[32,256,128]{2,1,0:T(8,128)(2,1)}), bf16[32,256,128]{2,1,0:T(8,128)(2,1)}, u32[]{:S(2)}, u32[]{:S(2)}) async-start(bf16[32,256,128]{2,1,0:T(8,128)(2,1)} %gather_fusion.1), calls=%async_computation.1 | async-start | bytes 4194304 | tf_op jit(solution)/shard_map/all_to_all | solution.py:224
  37.1 13.2 %collective-permute-start.3 = (bf16[2,128,2,512]{3,2,1,0:T(2,128)(2,1)}, bf16[2,128,2,512]{3,2,1,0:T(2,128)(2,1)S(1)}, u32[]{:S(2)}, u32[]{:S(2)}) collective-permute-start(bf16[2,128,2,512]{3,2,1,0:T(2,128)(2,1)} %get-tuple-element.49), channel_id=1, source_target_pairs={{0,192},{32,96},{64,128},{96,32},{128,64},{160,224},{192,0},{224,1... | collective-permute-start | bytes 1572872 | tf_op jit(solution)/shard_map/ppermute | solution.py:200
  42.9 0.9 copy-start.3
  43.8 7.5 %collective-permute-start.10 = (bf16[128,2,512]{2,1,0:T(2,128)(2,1)S(1)}, bf16[128,2,512]{2,1,0:T(2,128)(2,1)S(1)}, u32[]{:S(2)}, u32[]{:S(2)}) collective-permute-start(bf16[128,2,512]{2,1,0:T(2,128)(2,1)S(1)} %get-tuple-element.58), channel_id=1, source_target_pairs={{0,192},{32,96},{64,128},{96,32},{128,64},{160,224},{192,0},{224,1... | collective-permute-start | bytes 786440 | tf_op jit(solution)/shard_map/ppermute | solution.py:200
  43.9 53.7 %collective-permute-start.4 = (bf16[3,128,2,512]{3,2,1,0:T(2,128)(2,1)}, bf16[3,128,2,512]{3,2,1,0:T(2,128)(2,1)S(1)}, u32[]{:S(2)}, u32[]{:S(2)}) collective-permute-start(bf16[3,128,2,512]{3,2,1,0:T(2,128)(2,1)} %get-tuple-element.52), channel_id=1, source_target_pairs={{0,160},{32,128},{64,224},{96,192},{128,32},{160,0},{192,96},{224,... | collective-permute-start | bytes 2359304 | tf_op jit(solution)/shard_map/ppermute | solution.py:200
  48.5 50.0 %collective-permute-start.5 = (bf16[3,128,2,512]{3,2,1,0:T(2,128)(2,1)}, bf16[3,128,2,512]{3,2,1,0:T(2,128)(2,1)}, u32[]{:S(2)}, u32[]{:S(2)}) collective-permute-start(bf16[3,128,2,512]{3,2,1,0:T(2,128)(2,1)} %get-tuple-element.53), channel_id=1, source_target_pairs={{0,96},{32,192},{64,32},{96,128},{128,224},{160,64},{192,160},{224... | collective-permute-start | bytes 2359304 | tf_op jit(solution)/shard_map/ppermute | solution.py:200
  49.6 48.9 %collective-permute-start.6 = (bf16[3,128,2,512]{3,2,1,0:T(2,128)(2,1)}, bf16[3,128,2,512]{3,2,1,0:T(2,128)(2,1)}, u32[]{:S(2)}, u32[]{:S(2)}) collective-permute-start(bf16[3,128,2,512]{3,2,1,0:T(2,128)(2,1)} %get-tuple-element.54), channel_id=1, source_target_pairs={{0,224},{32,64},{64,160},{96,0},{128,96},{160,192},{192,32},{224,1... | collective-permute-start | bytes 2359304 | tf_op jit(solution)/shard_map/ppermute | solution.py:200
  50.3 0.8 copy-start.7
  51.1 47.4 %collective-permute-start.7 = (bf16[3,128,2,512]{3,2,1,0:T(2,128)(2,1)}, bf16[3,128,2,512]{3,2,1,0:T(2,128)(2,1)}, u32[]{:S(2)}, u32[]{:S(2)}) collective-permute-start(bf16[3,128,2,512]{3,2,1,0:T(2,128)(2,1)} %get-tuple-element.55), channel_id=1, source_target_pairs={{0,32},{32,0},{64,96},{96,64},{128,160},{160,128},{192,224},{224,1... | collective-permute-start | bytes 2359304 | tf_op jit(solution)/shard_map/ppermute | solution.py:200
  51.3 0.7 copy-start.9
  52.0 38.1 %collective-permute-start.8 = (bf16[128,2,512]{2,1,0:T(2,128)(2,1)S(1)}, bf16[128,2,512]{2,1,0:T(2,128)(2,1)S(1)}, u32[]{:S(2)}, u32[]{:S(2)}) collective-permute-start(bf16[128,2,512]{2,1,0:T(2,128)(2,1)S(1)} %get-tuple-element.56), channel_id=1, source_target_pairs={{0,128},{32,160},{64,192},{96,224},{128,0},{160,32},{192,64},{224,... | collective-permute-start | bytes 786440 | tf_op jit(solution)/shard_map/ppermute | solution.py:200
  90.2 0.7 copy-start.11
  90.9 6.7 %collective-permute-start.9 = (bf16[128,2,512]{2,1,0:T(2,128)(2,1)}, bf16[128,2,512]{2,1,0:T(2,128)(2,1)}, u32[]{:S(2)}, u32[]{:S(2)}) collective-permute-start(bf16[128,2,512]{2,1,0:T(2,128)(2,1)} %get-tuple-element.57), channel_id=1, source_target_pairs={{0,64},{32,224},{64,0},{96,160},{128,192},{160,96},{192,128},{224,... | collective-permute-start | bytes 786440 | tf_op jit(solution)/shard_map/ppermute | solution.py:200
  97.6 0.9 copy-start.5
  98.5 9.2 %copy-start.4 = (bf16[3,128,2,512]{3,2,1,0:T(2,128)(2,1)S(1)}, bf16[3,128,2,512]{3,2,1,0:T(2,128)(2,1)}, u32[]{:S(2)}) copy-start(bf16[3,128,2,512]{3,2,1,0:T(2,128)(2,1)} %copy-done.3) | copy-start | bytes 2359300
  98.5 45.8 %all-to-all-start.2 = ((bf16[16,3,256,128]{3,2,1,0:T(8,128)(2,1)}), bf16[16,3,256,128]{3,2,1,0:T(8,128)(2,1)}, u32[]{:S(2)}, u32[]{:S(2)}) async-start(bf16[16,3,256,128]{3,2,1,0:T(8,128)(2,1)} %shard_map.47), calls=%async_computation.2 | async-start | bytes 6291456 | tf_op jit(solution)/shard_map/all_to_all | solution.py:250
  107.7 1.1 copy-start.6
  108.9 1.0 copy-start.8
  109.9 0.9 copy-start.10
  110.9 0.9 copy-start.12
  115.5 2.6 %copy-start.1 = (bf16[3,2,1024,512]{3,2,1,0:T(8,128)(2,1)}, bf16[3,2,1024,512]{3,2,1,0:T(8,128)(2,1)S(1)}, u32[]{:S(2)}) copy-start(bf16[3,2,1024,512]{3,2,1,0:T(8,128)(2,1)S(1)} %shard_map.49.table) | copy-start | bytes 18874372
  151.3 26.4 %all-to-all-start.3 = ((bf16[16,3,2,64,128]{4,3,2,1,0:T(8,128)(2,1)}), bf16[16,3,2,64,128]{4,3,2,1,0:T(8,128)(2,1)}, u32[]{:S(2)}, u32[]{:S(2)}) async-start(bf16[16,3,2,64,128]{4,3,2,1,0:T(8,128)(2,1)} %shard_map.50), calls=%async_computation.3 | async-start | bytes 3145728 | tf_op jit(solution)/shard_map/all_to_all | solution.py:281
